TPU v7x, 512 devices: a whole 4x4x16 slice. The times are simulated.
512 devices in a mesh: var: 8 (over z_lo), lat: 64 (over z_hi, x, y, core).
Axes of the slice: x: 4, y: 4, z: 16 (z_hi: 2, z_lo: 8; z = z_hi * 8 + z_lo), core: 2. Of those that a mesh axis runs over, the one named last changes fastest.
Arguments:
- fields: bfloat16 [64, 1536, 384], P('var', 'lat'), may hold values from -6 to 6
- field_ids: int32 [64], replicated, may hold values from 0 to 63, each once
- embed_w: bfloat16 [64, 16, 512], replicated, may hold values from -1.5 to 1.5
- lat_query: bfloat16 [4, 512], replicated, may hold values from -3 to 3
- perc_wk: bfloat16 [512, 512], replicated, may hold values from -10 to 10
- perc_wv: bfloat16 [512, 512], replicated, may hold values from -0.25 to 0.25
- swin_qkv: bfloat16 [512, 1536], replicated, may hold values from -12 to 12
- swin_wo: bfloat16 [512, 512], replicated, may hold values from -0.25 to 0.25
- row_window: int32 [384], replicated, may hold values from 0 to 127, never falling along the last dimension, each value on 1 to 6 neighbouring positions
- lon_shift: int32 [2], replicated, may hold values from 1 to 11, as said below
Outputs:
- encoded: bfloat16 [4, 384, 96, 512], P(None, 'lat', 'var')
Inputs may be any that keep to these rules, and one draw needn't show every extreme that they name: `row_window`: window ids never fall along the rows, and one id covers at most 6 consecutive rows; some id covers exactly 6. `lon_shift`: the shifts are distinct, and the largest is exactly 11.
All inputs are finite; a program needn't handle non-finite values.
Results may differ from a plain program's by a relative error of at most 0.019.
The roundings to bfloat16 on the way count: a program that leaves them out, or rounds other values in their place, can miss the bound.
Values may be sent and summed in bfloat16 or wider, within the bound.
A program may use at most 64 MiB of HBM per device.

v0:
```python
import math

import jax
import jax.numpy as jnp
from jax import lax
from jax.experimental import pallas as pl
from jax.experimental.pallas import tpu as pltpu
from jax.sharding import PartitionSpec as P

D = 512
HEADS = 16
HEAD = 32
LEVELS = 4
PATCH = 4
WIN_LAT = 6
WIN_LON = 12
FIELDS = 64
ROWS = 6
COLS = 12
PIX = PATCH * PATCH
GROUP = 4
QUADS = COLS // GROUP
LINE = 2 * COLS
OWN = ROWS * LINE
HALO = 128
KEYS = 384
EDGE = 120

EPSILON = 1e-05
MASKED = -1e30
EXP2_SCALE = math.log2(math.e) / math.sqrt(HEAD)
F32 = jnp.float32
BF16 = jnp.bfloat16
NT = (((1,), (1,)), ((), ()))


def dot(a, b):
    return jnp.dot(a, b, preferred_element_type=F32)


def iota(shape, dim):
    return lax.broadcasted_iota(jnp.int32, shape, dim)


def layer_norm(values):
    row_mean = jnp.sum(values, axis=-1, keepdims=True) * (1.0 / D)
    centred = values - row_mean
    variance = jnp.sum(centred * centred, axis=-1, keepdims=True) * (1.0 / D)
    return centred * lax.rsqrt(variance + EPSILON)


def softmax_rows(scores):
    row_top = jnp.max(scores, axis=-1, keepdims=True)
    lifted = jnp.exp2(scores - row_top)
    return lifted * (1.0 / jnp.sum(lifted, axis=-1, keepdims=True))


def encode_kernel(
    ids_ref, shift_ref, pix_ref, embed_ref, query_ref, wk_ref, wv_ref, out_ref,
    slot_w, keys_scr, bias_scr, normed_scr, pooled_scr, query_scr,
):
    step = pl.program_id(0)

    @pl.when(step == 0)
    def _():
        def place(slot, carry):
            start = pl.multiple_of(slot * PIX, PIX)
            slot_w[pl.ds(start, PIX), :] = embed_ref[ids_ref[slot]]
            return carry

        lax.fori_loop(0, FIELDS, place, 0)
        swap = shift_ref[1] > shift_ref[0]
        query = query_ref[...].astype(F32)
        swapped = jnp.concatenate([query[2:], query[:2]], axis=0)
        query = jnp.where(swap, swapped, query)
        row = iota((256, D), 0)
        level = (row // GROUP) % LEVELS
        spread = jnp.zeros((256, D), F32)
        for lev in range(LEVELS):
            spread = jnp.where(level == lev, query[lev : lev + 1, :], spread)
        query_scr[...] = spread[:16]
        own_head = iota((256, D), 1) // HEAD == row // 16
        masked = jnp.where(own_head, spread, 0.0).astype(BF16)
        keys_scr[...] = lax.dot_general(
            masked, wk_ref[...], NT, preferred_element_type=F32
        ).astype(BF16)
        same = iota((256, 256), 1) // FIELDS == iota((256, 256), 0) % GROUP
        bias_scr[...] = jnp.where(same, 0.0, MASKED)

    own_slot = iota((1, 16, 256), 2) // PIX == iota((1, 16, 256), 1)
    for part in range(4):
        pixels = jnp.concatenate(
            [pix_ref[2 * part, 0], pix_ref[2 * part + 1, 0]], axis=-1
        ).astype(F32)
        spread = jnp.where(own_slot, pixels[:, None, :], 0.0).astype(BF16)
        tokens = dot(spread.reshape(COLS * 16, 256), slot_w[256 * part : 256 * part + 256, :])
        normed = layer_norm(tokens.astype(BF16).astype(F32)).astype(BF16)
        normed_scr[:, 16 * part : 16 * part + 16, :] = normed.reshape(COLS, 16, D)
    for quad in range(QUADS):
        normed = normed_scr[GROUP * quad : GROUP * quad + GROUP].reshape(GROUP * FIELDS, D)
        scores = lax.dot_general(keys_scr[...], normed, NT, preferred_element_type=F32)
        weights = softmax_rows(scores * EXP2_SCALE + bias_scr[...]).astype(BF16)
        pooled = dot(weights, normed).astype(BF16)
        start = pl.multiple_of(step * 48 + quad * 16, 16)
        pooled_scr[:, pl.ds(start, 16), :] = pooled.reshape(HEADS, 16, D)

    @pl.when(step == ROWS - 1)
    def _():
        halves = []
        for half in range(2):
            lane_head = iota((D, 256), 1) // HEAD
            value_w = wv_ref[:, 256 * half : 256 * half + 256].astype(F32)
            total = jnp.zeros((2 * OWN, 256), F32)
            for head in range(8):
                masked = jnp.where(lane_head == head, value_w, 0.0).astype(BF16)
                total = total + dot(pooled_scr[8 * half + head], masked)
            halves.append(total)
        projected = jnp.concatenate(halves, axis=-1).reshape(ROWS * QUADS, 16, D)
        latents = projected + query_scr[...][None]
        for pair in range(2):
            out_ref[pair] = latents[:, 8 * pair : 8 * pair + 8].reshape(OWN, D).astype(BF16)


def encode(ids, shift, pixels, embed_w, lat_query, wk, wv):
    vmem = pl.BlockSpec(memory_space=pltpu.VMEM)
    smem = pl.BlockSpec(memory_space=pltpu.SMEM)
    return pl.pallas_call(
        encode_kernel,
        out_shape=jax.ShapeDtypeStruct((2, OWN, D), BF16),
        grid=(ROWS,),
        in_specs=[
            smem, smem,
            pl.BlockSpec((8, 1, COLS, 128), lambda r: (0, r, 0, 0)),
            vmem, vmem, vmem, vmem,
        ],
        out_specs=vmem,
        scratch_shapes=[
            pltpu.VMEM((FIELDS * PIX, D), BF16),
            pltpu.VMEM((256, D), BF16),
            pltpu.VMEM((256, 256), F32),
            pltpu.VMEM((COLS, FIELDS, D), BF16),
            pltpu.VMEM((HEADS, 2 * OWN, D), BF16),
            pltpu.VMEM((16, D), F32),
        ],
        compiler_params=pltpu.CompilerParams(vmem_limit_bytes=48 << 20),
        name="encode",
    )(ids, shift, pixels, embed_w, lat_query, wk, wv)


def column_of(token):
    return (token % LINE) // 8 * GROUP + token % GROUP


def attend_kernel(window_ref, shift_ref, own_ref, up_ref, down_ref, qkv_ref, wo_ref, out_ref):
    sector = lax.axis_index("var")
    sectors = lax.axis_size("var")
    first = lax.axis_index("lat") * ROWS - (WIN_LAT - 1)
    total_rows = window_ref.shape[0]
    shift = jnp.minimum(shift_ref[0], shift_ref[1])
    key_token = iota((1, KEYS), 1)
    query_token = iota((OWN, 1), 0)
    key_row = jnp.full((1, KEYS), -1, jnp.int32)
    query_row = jnp.full((OWN, 1), -1, jnp.int32)
    for k in range(ROWS + 2 * (WIN_LAT - 1)):
        row = first + k
        inside = (row >= 0) & (row < total_rows)
        ident = jnp.where(inside, window_ref[jnp.clip(row, 0, total_rows - 1)], -1)
        key_row = jnp.where(key_token // LINE == k, ident, key_row)
        if 0 <= k - (WIN_LAT - 1) < ROWS:
            query_row = jnp.where(query_token // LINE == k - (WIN_LAT - 1), ident, query_row)

    for pair in range(2):
        def wrapped(token):
            column = column_of(token)
            if pair == 0:
                return jnp.where((column == COLS - 1) & (sector == 0), 1, 0)
            return jnp.where((column < shift) & (sector == sectors - 1), 1, 0)

        same = (query_row * 2 + wrapped(query_token)) == (key_row * 2 + wrapped(key_token))
        bias = jnp.where(same, 0.0, MASKED)
        own = own_ref[pair].astype(F32)
        up = up_ref[pair].astype(F32)[HALO - EDGE :]
        down = down_ref[pair].astype(F32)[:EDGE]
        normed = layer_norm(jnp.concatenate([up, own, down], axis=0))
        queries = dot(normed[EDGE : EDGE + OWN].astype(BF16), qkv_ref[:, :D])
        normed = normed.astype(BF16)
        keys = dot(normed, qkv_ref[:, D : 2 * D]).astype(BF16)
        values = dot(normed, qkv_ref[:, 2 * D :]).astype(BF16)
        halves = []
        lane_head = iota((OWN, 256), 1) // HEAD
        for half in range(2):
            cut = slice(256 * half, 256 * half + 256)
            part = queries[:, cut]
            stacked = jnp.concatenate(
                [jnp.where(lane_head == h, part, 0.0).astype(BF16) for h in range(8)], axis=0
            )
            scores = lax.dot_general(stacked, keys[:, cut], NT, preferred_element_type=F32)
            scores = scores.reshape(8, OWN, KEYS) * EXP2_SCALE + bias[None]
            weights = softmax_rows(scores).astype(BF16).reshape(8 * OWN, KEYS)
            mixed = dot(weights, values[:, cut]).reshape(8, OWN, 256)
            total = jnp.zeros((OWN, 256), F32)
            for h in range(8):
                total = jnp.where(lane_head == h, mixed[h], total)
            halves.append(total.astype(BF16))
        update = dot(jnp.concatenate(halves, axis=-1), wo_ref[...])
        out_ref[pair] = (own + update).astype(BF16)


def attend(window, shift, own, up, down, qkv, wo):
    vmem = pl.BlockSpec(memory_space=pltpu.VMEM)
    smem = pl.BlockSpec(memory_space=pltpu.SMEM)
    return pl.pallas_call(
        attend_kernel,
        out_shape=jax.ShapeDtypeStruct((2, OWN, D), BF16),
        in_specs=[smem, smem] + [vmem] * 5,
        out_specs=vmem,
        compiler_params=pltpu.CompilerParams(vmem_limit_bytes=48 << 20),
        name="attend",
    )(window, shift, own, up, down, qkv, wo)


def shards(
    fields, field_ids, embed_w, lat_query, perc_wk, perc_wv, swin_qkv, swin_wo, row_window, lon_shift
):
    sectors = lax.axis_size("var")
    bands = lax.axis_size("lat")
    blocks = fields.reshape(8, ROWS, PATCH, sectors, COLS, PATCH)
    blocks = jnp.transpose(blocks, (3, 1, 4, 0, 2, 5)).reshape(sectors, ROWS, COLS, 128)
    pixels = lax.all_to_all(blocks, "var", split_axis=0, concat_axis=0, tiled=True)
    latents = encode(field_ids, lon_shift, pixels, embed_w, lat_query, perc_wk, perc_wv)

    shift = jnp.minimum(lon_shift[0], lon_shift[1])
    split = latents.reshape(2, ROWS, QUADS, 2, GROUP, D)
    rightward = [(i, (i + 1) % sectors) for i in range(sectors)]
    leftward = [((i + 1) % sectors, i) for i in range(sectors)]
    from_left = lax.ppermute(split[0, :, 2:], "var", rightward)
    from_right = lax.ppermute(split[1], "var", leftward)
    column = (
        lax.broadcasted_iota(jnp.int32, (1, QUADS, 1, GROUP, 1), 1) * GROUP
        + lax.broadcasted_iota(jnp.int32, (1, QUADS, 1, GROUP, 1), 3)
    )
    from_left = jnp.broadcast_to(from_left, split[0].shape)
    slab = jnp.stack(
        [
            jnp.where(column == COLS - 1, from_left, split[0]),
            jnp.where(column < shift, from_right, split[1]),
        ]
    ).reshape(2, OWN, D)

    downward = [(i, i + 1) for i in range(bands - 1)]
    upward = [(i + 1, i) for i in range(bands - 1)]
    up = lax.ppermute(slab[:, OWN - HALO :], "lat", downward)
    down = lax.ppermute(slab[:, :HALO], "lat", upward)
    encoded = attend(row_window, lon_shift, slab, up, down, swin_qkv, swin_wo)

    split = encoded.reshape(2, ROWS, QUADS, 2, GROUP, D)
    back_left = lax.ppermute(split[0, :, 2:], "var", leftward)
    back_right = lax.ppermute(split[1], "var", rightward)
    back_left = jnp.broadcast_to(back_left, split[0].shape)
    pairs = jnp.stack(
        [
            jnp.where(column == COLS - 1, back_left, split[0]),
            jnp.where(column < shift, back_right, split[1]),
        ]
    )
    pairs = jnp.where(lon_shift[1] > lon_shift[0], pairs[::-1], pairs)
    return jnp.transpose(pairs, (0, 3, 1, 2, 4, 5)).reshape(LEVELS, ROWS, COLS, D)


def solution(mesh):
    in_specs = (P("var", "lat", None), P(), P(), P(), P(), P(), P(), P(), P(), P())
    out_specs = P(None, "lat", "var", None)
    return jax.shard_map(shards, mesh=mesh, in_specs=in_specs, out_specs=out_specs, check_vma=False)
```

profile of v0, /device:TPU:31, one launch (start us, length us, event | category | flops | bytes accessed | tf_op | source)
XLA Modules:
  0.0 133.2 jit_solution(3826450756057184093)
XLA Ops:
  0.0 2.4 %copy.13 = bf16[8,24,384]{0,2,1:T(8,128)(2,1)S(1)} copy(bf16[8,24,384]{2,1,0:T(8,128)(2,1)} %param.10) | data formatting | bytes 294912 | tf_op args[0]
  2.4 6.8 %copy.14 = bf16[8,6,12,8,4,4]{2,0,5,4,3,1:T(8,128)(2,1)} copy(bf16[8,6,12,8,4,4]{3,5,2,0,4,1:T(4,128)(2,1)S(1)} %bitcast.18) | data formatting | bytes 294912 | tf_op jit(solution)/shard_map/transpose | solution.py:228
  9.1 0.0 copy-start.5
  9.1 0.0 copy-start.1
  9.1 0.0 copy-start.6
  9.1 0.0 copy-start.8
  9.2 3.1 %copy.15 = bf16[8,6,12,128]{3,2,1,0:T(8,128)(2,1)} copy(bf16[8,6,12,128]{2,0,3,1:T(8,128)(2,1)} %bitcast.19) | data formatting | bytes 294912 | tf_op jit(solution)/shard_map/reshape | solution.py:228
  12.2 12.2 %all-to-all-start = ((bf16[8,6,12,128]{3,2,1,0:T(8,128)(2,1)}), bf16[8,6,12,128]{3,2,1,0:T(8,128)(2,1)S(1)}, u32[]{:S(2)}, u32[]{:S(2)}) async-start(bf16[8,6,12,128]{3,2,1,0:T(8,128)(2,1)} %copy.15), calls=%async_computation | async-start | bytes 393216 | tf_op jit(solution)/shard_map/all_to_all | solution.py:229
  24.5 0.0 copy-done.5
  24.5 0.6 fusion.6
  26.4 9.2 %all-to-all-done.pix_ref = bf16[8,6,12,128]{3,2,1,0:T(8,128)(2,1)S(1)} async-done(((bf16[8,6,12,128]{3,2,1,0:T(8,128)(2,1)}), bf16[8,6,12,128]{3,2,1,0:T(8,128)(2,1)S(1)}, u32[]{:S(2)}, u32[]{:S(2)}) %all-to-all-start) | async-done | bytes 147488 | tf_op jit(solution)/shard_map/all_to_all | solution.py:229
  35.6 0.0 copy-done.1
  35.6 0.0 copy-done.2
  35.6 0.0 copy-done.3
  35.6 0.0 copy-done.6
  35.6 0.0 copy-done.8
  35.6 15.3 %encode.1 = bf16[2,144,512]{2,1,0:T(8,128)(2,1)S(1)} custom-call(s32[64]{0:T(128)S(1)} %copy-done.8, s32[2]{0:T(128)S(1)} %copy-done.5, bf16[8,6,12,128]{3,2,1,0:T(8,128)(2,1)S(1)} %all-to-all-done.pix_ref, bf16[64,16,512]{2,1,0:T(8,128)(2,1)S(1)} %copy-done.1, bf16[4,512]{1,0:T(4,128)(2,1)S(1)} %copy-done.6, bf16[512,512]{1,0:T(8,128)(2,1)S(1)} %copy-done.2, ...), custom_call_target="tpu_custom_call" | custom-call | tf_op jit(solution)/shard_map/encode/pallas_call | solution.py:127
  50.9 0.1 reshape.80
  51.0 1.9 %collective-permute-start = (bf16[6,1,2,4,512]{4,3,2,0,1:T(4,128)(2,1)S(1)}, bf16[6,1,2,4,512]{4,3,2,0,1:T(4,128)(2,1)S(1)}, u32[]{:S(2)}, u32[]{:S(2)}) collective-permute-start(bf16[6,1,2,4,512]{4,3,2,0,1:T(4,128)(2,1)S(1)} %slice_bitcast_fusion.1), channel_id=1, source_target_pairs={{0,64},{64,128},{128,192},{192,256},{256,320},{320,384},{384,448},... | collective-permute-start | bytes 147464 | tf_op jit(solution)/shard_map/ppermute | solution.py:236
  53.0 0.1 fusion.4
  53.0 0.1 broadcast_in_dim.43
  53.2 9.4 %collective-permute-done = bf16[6,1,2,4,512]{4,3,2,0,1:T(4,128)(2,1)S(1)} collective-permute-done((bf16[6,1,2,4,512]{4,3,2,0,1:T(4,128)(2,1)S(1)}, bf16[6,1,2,4,512]{4,3,2,0,1:T(4,128)(2,1)S(1)}, u32[]{:S(2)}, u32[]{:S(2)}) %collective-permute-start) | collective-permute-done | bytes 49184 | tf_op jit(solution)/shard_map/ppermute | solution.py:236
  62.7 0.0 copy-start
  62.7 0.0 copy-start.4
  62.7 0.0 copy-start.7
  62.7 0.1 slice_select_fusion
  62.8 2.1 %collective-permute-start.1 = (bf16[6,3,2,4,512]{4,3,2,1,0:T(4,128)(2,1)S(1)}, bf16[6,3,2,4,512]{4,3,2,1,0:T(4,128)(2,1)S(1)}, u32[]{:S(2)}, u32[]{:S(2)}) collective-permute-start(bf16[6,3,2,4,512]{4,3,2,1,0:T(4,128)(2,1)S(1)} %squeeze.11), channel_id=1, source_target_pairs={{64,0},{128,64},{192,128},{256,192},{320,256},{384,320},{448,384},... | collective-permute-start | bytes 442376 | tf_op jit(solution)/shard_map/ppermute | solution.py:237
  64.9 4.0 %collective-permute-done.1 = bf16[6,3,2,4,512]{4,3,2,1,0:T(4,128)(2,1)S(1)} collective-permute-done((bf16[6,3,2,4,512]{4,3,2,1,0:T(4,128)(2,1)S(1)}, bf16[6,3,2,4,512]{4,3,2,1,0:T(4,128)(2,1)S(1)}, u32[]{:S(2)}, u32[]{:S(2)}) %collective-permute-start.1) | collective-permute-done | bytes 147488 | tf_op jit(solution)/shard_map/ppermute | solution.py:237
  68.9 0.1 broadcast_select_fusion
  69.1 13.8 %collective-permute-start.2 = (bf16[2,128,512]{2,1,0:T(8,128)(2,1)S(1)}, bf16[2,128,512]{2,1,0:T(8,128)(2,1)S(1)}, u32[]{:S(2)}, u32[]{:S(2)}) collective-permute-start(bf16[2,128,512]{2,1,0:T(8,128)(2,1)S(1)} %get-tuple-element.8), channel_id=1, source_target_pairs={{0,1},{1,2},{2,3},{3,4},{4,5},{5,6},{6,7},{7,8},{8,9},{9,10},{10,1... | collective-permute-start | bytes 786440 | tf_op jit(solution)/shard_map/ppermute | solution.py:252
  82.9 1.9 %collective-permute-start.3 = (bf16[2,128,512]{2,1,0:T(8,128)(2,1)S(1)}, bf16[2,128,512]{2,1,0:T(8,128)(2,1)S(1)}, u32[]{:S(2)}, u32[]{:S(2)}) collective-permute-start(bf16[2,128,512]{2,1,0:T(8,128)(2,1)S(1)} %get-tuple-element.7), channel_id=1, source_target_pairs={{1,0},{2,1},{3,2},{4,3},{5,4},{6,5},{7,6},{8,7},{9,8},{10,9},{11,1... | collective-permute-start | bytes 786440 | tf_op jit(solution)/shard_map/ppermute | solution.py:253
  86.1 0.1 collective-permute-done.2.up_ref
  86.2 17.5 %collective-permute-done.3.down_ref = bf16[2,128,512]{2,1,0:T(8,128)(2,1)S(1)} collective-permute-done((bf16[2,128,512]{2,1,0:T(8,128)(2,1)S(1)}, bf16[2,128,512]{2,1,0:T(8,128)(2,1)S(1)}, u32[]{:S(2)}, u32[]{:S(2)}) %collective-permute-start.3) | collective-permute-done | bytes 262176 | tf_op jit(solution)/shard_map/ppermute | solution.py:253
  103.6 0.0 copy-done
  103.6 0.0 copy-done.4
  103.6 0.0 copy-done.7
  103.6 6.6 %attend.1 = bf16[2,144,512]{2,1,0:T(8,128)(2,1)S(1)} custom-call(s32[384]{0:T(512)S(1)} %copy-done.7, s32[2]{0:T(128)S(1)} %copy-done.5, bf16[2,144,512]{2,1,0:T(8,128)(2,1)S(1)} %pad_maximum_fusion.own_ref, bf16[2,128,512]{2,1,0:T(8,128)(2,1)S(1)} %collective-permute-done.2.up_ref, bf16[2,128,512]{2,1,0:T(8,128)(2,1)S(1)} %collective-permute-done.3.down_ref, ...), custom_call_target="tpu_custom_call" | custom-call | tf_op jit(solution)/shard_map/attend/pallas_call | solution.py:212
  110.3 0.1 reshape.81
  110.4 8.6 %collective-permute-start.4 = (bf16[6,1,2,4,512]{4,3,2,0,1:T(4,128)(2,1)S(1)}, bf16[6,1,2,4,512]{4,3,2,0,1:T(4,128)(2,1)S(1)}, u32[]{:S(2)}, u32[]{:S(2)}) collective-permute-start(bf16[6,1,2,4,512]{4,3,2,0,1:T(4,128)(2,1)S(1)} %slice_bitcast_fusion), channel_id=1, source_target_pairs={{64,0},{128,64},{192,128},{256,192},{320,256},{384,320},{448,384},... | collective-permute-start | bytes 147464 | tf_op jit(solution)/shard_map/ppermute | solution.py:257
  119.1 1.9 %collective-permute-start.5 = (bf16[6,3,2,4,512]{4,3,2,1,0:T(4,128)(2,1)S(1)}, bf16[6,3,2,4,512]{4,3,2,1,0:T(4,128)(2,1)S(1)}, u32[]{:S(2)}, u32[]{:S(2)}) collective-permute-start(bf16[6,3,2,4,512]{4,3,2,1,0:T(4,128)(2,1)S(1)} %squeeze.26), channel_id=1, source_target_pairs={{0,64},{64,128},{128,192},{192,256},{256,320},{320,384},{384,448},... | collective-permute-start | bytes 442376 | tf_op jit(solution)/shard_map/ppermute | solution.py:258
  121.1 0.0 collective-permute-done.4
  121.1 0.1 broadcast_select_fusion.1
  121.2 10.4 %collective-permute-done.5 = bf16[6,3,2,4,512]{4,3,2,1,0:T(4,128)(2,1)S(1)} collective-permute-done((bf16[6,3,2,4,512]{4,3,2,1,0:T(4,128)(2,1)S(1)}, bf16[6,3,2,4,512]{4,3,2,1,0:T(4,128)(2,1)S(1)}, u32[]{:S(2)}, u32[]{:S(2)}) %collective-permute-start.5) | collective-permute-done | bytes 147488 | tf_op jit(solution)/shard_map/ppermute | solution.py:258
  131.6 0.1 select_bitcast_fusion
  131.8 0.2 pad_maximum_fusion.1
  132.0 0.1 fusion
  132.1 0.3 copy.16
  132.4 0.8 reshape.82
  (15 shorter events, 0.4 us)
Async XLA Ops:
  9.1 15.4 %copy-start.5 = (s32[2]{0:T(128)S(1)}, s32[2]{0:T(128)}, u32[]{:S(2)}) copy-start(s32[2]{0:T(128)} %shift_ref.3) | copy-start | bytes 28
  9.1 26.5 %copy-start.1 = (bf16[64,16,512]{2,1,0:T(8,128)(2,1)S(1)}, bf16[64,16,512]{2,1,0:T(8,128)(2,1)}, u32[]{:S(2)}) copy-start(bf16[64,16,512]{2,1,0:T(8,128)(2,1)} %embed_ref.1) | copy-start | bytes 3145732
  9.1 26.5 %copy-start.2 = (bf16[512,512]{1,0:T(8,128)(2,1)S(1)}, bf16[512,512]{1,0:T(8,128)(2,1)}, u32[]{:S(2)}) copy-start(bf16[512,512]{1,0:T(8,128)(2,1)} %wk_ref.1) | copy-start | bytes 1572868
  9.1 26.5 %copy-start.3 = (bf16[512,512]{1,0:T(8,128)(2,1)S(1)}, bf16[512,512]{1,0:T(8,128)(2,1)}, u32[]{:S(2)}) copy-start(bf16[512,512]{1,0:T(8,128)(2,1)} %wv_ref.1) | copy-start | bytes 1572868
  9.1 26.5 %copy-start.6 = (bf16[4,512]{1,0:T(4,128)(2,1)S(1)}, bf16[4,512]{1,0:T(4,128)(2,1)}, u32[]{:S(2)}) copy-start(bf16[4,512]{1,0:T(4,128)(2,1)} %query_ref.1) | copy-start | bytes 12292
  9.1 26.5 %copy-start.8 = (s32[64]{0:T(128)S(1)}, s32[64]{0:T(128)}, u32[]{:S(2)}) copy-start(s32[64]{0:T(128)} %ids_ref.1) | copy-start | bytes 772
  12.2 23.4 %all-to-all-start = ((bf16[8,6,12,128]{3,2,1,0:T(8,128)(2,1)}), bf16[8,6,12,128]{3,2,1,0:T(8,128)(2,1)S(1)}, u32[]{:S(2)}, u32[]{:S(2)}) async-start(bf16[8,6,12,128]{3,2,1,0:T(8,128)(2,1)} %copy.15), calls=%async_computation | async-start | bytes 393216 | tf_op jit(solution)/shard_map/all_to_all | solution.py:229
  51.0 11.5 %collective-permute-start = (bf16[6,1,2,4,512]{4,3,2,0,1:T(4,128)(2,1)S(1)}, bf16[6,1,2,4,512]{4,3,2,0,1:T(4,128)(2,1)S(1)}, u32[]{:S(2)}, u32[]{:S(2)}) collective-permute-start(bf16[6,1,2,4,512]{4,3,2,0,1:T(4,128)(2,1)S(1)} %slice_bitcast_fusion.1), channel_id=1, source_target_pairs={{0,64},{64,128},{128,192},{192,256},{256,320},{320,384},{384,448},... | collective-permute-start | bytes 147464 | tf_op jit(solution)/shard_map/ppermute | solution.py:236
  62.7 41.0 %copy-start = (bf16[512,1536]{1,0:T(8,128)(2,1)S(1)}, bf16[512,1536]{1,0:T(8,128)(2,1)}, u32[]{:S(2)}) copy-start(bf16[512,1536]{1,0:T(8,128)(2,1)} %qkv_ref.1) | copy-start | bytes 4718596
  62.7 41.0 %copy-start.4 = (bf16[512,512]{1,0:T(8,128)(2,1)S(1)}, bf16[512,512]{1,0:T(8,128)(2,1)}, u32[]{:S(2)}) copy-start(bf16[512,512]{1,0:T(8,128)(2,1)} %wo_ref.1) | copy-start | bytes 1572868
  62.7 41.0 %copy-start.7 = (s32[384]{0:T(512)S(1)}, s32[384]{0:T(512)}, u32[]{:S(2)}) copy-start(s32[384]{0:T(512)} %window_ref.1) | copy-start | bytes 4612
  62.8 6.0 %collective-permute-start.1 = (bf16[6,3,2,4,512]{4,3,2,1,0:T(4,128)(2,1)S(1)}, bf16[6,3,2,4,512]{4,3,2,1,0:T(4,128)(2,1)S(1)}, u32[]{:S(2)}, u32[]{:S(2)}) collective-permute-start(bf16[6,3,2,4,512]{4,3,2,1,0:T(4,128)(2,1)S(1)} %squeeze.11), channel_id=1, source_target_pairs={{64,0},{128,64},{192,128},{256,192},{320,256},{384,320},{448,384},... | collective-permute-start | bytes 442376 | tf_op jit(solution)/shard_map/ppermute | solution.py:237
  69.1 17.1 %collective-permute-start.2 = (bf16[2,128,512]{2,1,0:T(8,128)(2,1)S(1)}, bf16[2,128,512]{2,1,0:T(8,128)(2,1)S(1)}, u32[]{:S(2)}, u32[]{:S(2)}) collective-permute-start(bf16[2,128,512]{2,1,0:T(8,128)(2,1)S(1)} %get-tuple-element.8), channel_id=1, source_target_pairs={{0,1},{1,2},{2,3},{3,4},{4,5},{5,6},{6,7},{7,8},{8,9},{9,10},{10,1... | collective-permute-start | bytes 786440 | tf_op jit(solution)/shard_map/ppermute | solution.py:252
  82.9 20.8 %collective-permute-start.3 = (bf16[2,128,512]{2,1,0:T(8,128)(2,1)S(1)}, bf16[2,128,512]{2,1,0:T(8,128)(2,1)S(1)}, u32[]{:S(2)}, u32[]{:S(2)}) collective-permute-start(bf16[2,128,512]{2,1,0:T(8,128)(2,1)S(1)} %get-tuple-element.7), channel_id=1, source_target_pairs={{1,0},{2,1},{3,2},{4,3},{5,4},{6,5},{7,6},{8,7},{9,8},{10,9},{11,1... | collective-permute-start | bytes 786440 | tf_op jit(solution)/shard_map/ppermute | solution.py:253
  110.4 10.7 %collective-permute-start.4 = (bf16[6,1,2,4,512]{4,3,2,0,1:T(4,128)(2,1)S(1)}, bf16[6,1,2,4,512]{4,3,2,0,1:T(4,128)(2,1)S(1)}, u32[]{:S(2)}, u32[]{:S(2)}) collective-permute-start(bf16[6,1,2,4,512]{4,3,2,0,1:T(4,128)(2,1)S(1)} %slice_bitcast_fusion), channel_id=1, source_target_pairs={{64,0},{128,64},{192,128},{256,192},{320,256},{384,320},{448,384},... | collective-permute-start | bytes 147464 | tf_op jit(solution)/shard_map/ppermute | solution.py:257
  119.1 12.5 %collective-permute-start.5 = (bf16[6,3,2,4,512]{4,3,2,1,0:T(4,128)(2,1)S(1)}, bf16[6,3,2,4,512]{4,3,2,1,0:T(4,128)(2,1)S(1)}, u32[]{:S(2)}, u32[]{:S(2)}) collective-permute-start(bf16[6,3,2,4,512]{4,3,2,1,0:T(4,128)(2,1)S(1)} %squeeze.26), channel_id=1, source_target_pairs={{0,64},{64,128},{128,192},{192,256},{256,320},{320,384},{384,448},... | collective-permute-start | bytes 442376 | tf_op jit(solution)/shard_map/ppermute | solution.py:258
where the time goes:
time: 134 us; the launch traced here: 133 us
  waiting for transfers between devices  50.5 us (38%)
  starting transfers between devices  42.5 us (32%)
  Pallas kernels  21.9 us (16%)
  local copies, waits for them, and re-layouts  14.5 us (11%)
  between operations  2.8 us (2%)
    ppermute x1, waiting for transfers between devices, shards(): down = lax.ppermute(slab[:, :HALO], 'lat', upward)  17.5 us
    pallas_call x1, Pallas kernels, encode(): pl.pallas_call(encode_kernel, out_shape=jax.ShapeDtypeStruct((2, OWN, D),...  15.3 us
    ppermute x1, starting transfers between devices, shards(): up = lax.ppermute(slab[:, OWN - HALO:], 'lat', downward)  13.8 us
    all_to_all x1, starting transfers between devices, shards(): lax.all_to_all(blocks, 'var', split_axis=0, concat_axis=0, tiled=True)  12.2 us
    ppermute x1, waiting for transfers between devices, shards(): back_right = lax.ppermute(split[1], 'var', rightward)  10.4 us
    ppermute x1, waiting for transfers between devices, shards(): from_left = lax.ppermute(split[0, :, 2:], 'var', rightward)  9.42 us
    all_to_all x1, waiting for transfers between devices, shards(): lax.all_to_all(blocks, 'var', split_axis=0, concat_axis=0, tiled=True)  9.23 us
    ppermute x1, starting transfers between devices, shards(): back_left = lax.ppermute(split[0, :, 2:], 'var', leftward)  8.65 us
  transfers between devices with their start and end apart: 7, of which 6 were waited for; matrix products, arithmetic and copies ran while one was open for 1% of the time, Pallas kernels for 0%

commit v1 on v0

v1 whole, which is shorter than its diff:
```python
import math

import jax
import jax.numpy as jnp
from jax import lax
from jax.experimental import pallas as pl
from jax.experimental.pallas import tpu as pltpu
from jax.sharding import PartitionSpec as P

D = 512
HEADS = 16
HEAD = 32
LEVELS = 4
PATCH = 4
WIN_LAT = 6
WIN_LON = 12
FIELDS = 64
ROWS = 6
COLS = 12
PIX = PATCH * PATCH
GROUP = 4
QUADS = COLS // GROUP
LINE = 2 * COLS
OWN = ROWS * LINE
HALO = 128
KEYS = 384
EDGE = 120

EPSILON = 1e-05
MASKED = -1e30
EXP2_SCALE = math.log2(math.e) / math.sqrt(HEAD)
F32 = jnp.float32
BF16 = jnp.bfloat16
NT = (((1,), (1,)), ((), ()))
MESH = pl.DeviceIdType.MESH
PIECES = ((0, 16), (16, 32), (48, 32))
SEND_ORDER = (4, 3, 5, 2, 6, 1, 7)
QUERY_PARTS = (((0, OWN),), ((0, 96), (96, OWN)))


def dot(a, b):
    return jnp.dot(a, b, preferred_element_type=F32)


def iota(shape, dim):
    return lax.broadcasted_iota(jnp.int32, shape, dim)


def layer_norm(values):
    row_mean = jnp.sum(values, axis=-1, keepdims=True) * (1.0 / D)
    centred = values - row_mean
    variance = jnp.sum(centred * centred, axis=-1, keepdims=True) * (1.0 / D)
    return centred * lax.rsqrt(variance + EPSILON)


def softmax_rows(scores):
    row_top = jnp.max(scores, axis=-1, keepdims=True)
    lifted = jnp.exp2(scores - row_top)
    return lifted * (1.0 / jnp.sum(lifted, axis=-1, keepdims=True))


def column_of(token):
    return (token % LINE) // 8 * GROUP + token % GROUP


def remote(src, dst, send_sem, recv_sem, **device):
    return pltpu.make_async_remote_copy(
        src_ref=src, dst_ref=dst, send_sem=send_sem, recv_sem=recv_sem,
        device_id=device, device_id_type=MESH,
    )


def attention(queries, keys, values, bias):
    count = queries.shape[0]
    lane_head = iota((count, 256), 1) // HEAD
    halves = []
    for half in range(2):
        cut = slice(256 * half, 256 * half + 256)
        part = queries[:, cut]
        stacked = jnp.concatenate(
            [jnp.where(lane_head == h, part, 0.0).astype(BF16) for h in range(8)], axis=0
        )
        scores = lax.dot_general(stacked, keys[:, cut], NT, preferred_element_type=F32)
        scores = scores.reshape(8, count, KEYS) * EXP2_SCALE + bias[None]
        weights = softmax_rows(scores).astype(BF16).reshape(8 * count, KEYS)
        mixed = dot(weights, values[:, cut]).reshape(8, count, 256)
        total = jnp.zeros((count, 256), F32)
        for h in range(8):
            total = jnp.where(lane_head == h, mixed[h], total)
        halves.append(total.astype(BF16))
    return jnp.concatenate(halves, axis=-1)


def pick_pixels(fields, stage, send):
    flat = fields.astype(F32).reshape(8 * ROWS * PATCH, 384).astype(BF16)
    row = iota((512, 1), 0)
    column = row % 16
    source = jnp.where(column < COLS, (row % 128) // 16 * 48 + column * PATCH + row // 128, -1)
    pick = jnp.where(source == iota((512, 384), 1), 1.0, 0.0).astype(BF16)
    turned = lax.dot_general(pick, flat, NT, preferred_element_type=F32).astype(BF16)
    row = iota((192, 1), 0)
    target = (row // PATCH) % ROWS * 128 + row // (ROWS * PATCH) * PIX + row % PATCH * PATCH
    lane = iota((192, 768), 1)
    total = jnp.zeros((128, 768), F32)
    for j in range(PATCH):
        place = jnp.where(target + j == lane, 1.0, 0.0).astype(BF16)
        total = total + dot(turned[128 * j : 128 * j + 128], place)
    for sector in range(8):
        stage[sector, 72:80, :] = jnp.zeros((8, 128), F32)
        for line in range(ROWS):
            stage[sector, COLS * line : COLS * line + COLS, :] = total[
                16 * sector : 16 * sector + COLS, 128 * line : 128 * line + 128
            ]
    send[...] = stage[...].astype(BF16)


def prepare_weights(ids_ref, shift_ref, embed, query_ref, wk, slot_w, keys_scr, bias_scr, query_scr):
    def place(slot, carry):
        start = pl.multiple_of(slot * PIX, PIX)
        slot_w[pl.ds(start, PIX), :] = embed[ids_ref[slot]]
        return carry

    lax.fori_loop(0, FIELDS, place, 0)
    swap = shift_ref[1] > shift_ref[0]
    query = query_ref[...].astype(F32)
    swapped = jnp.concatenate([query[2:], query[:2]], axis=0)
    query = jnp.where(swap, swapped, query)
    level = (iota((256, D), 0) // GROUP) % LEVELS
    spread = jnp.zeros((256, D), F32)
    for lev in range(LEVELS):
        spread = jnp.where(level == lev, query[lev : lev + 1, :], spread)
    query_scr[...] = spread[:16]
    own_head = iota((256, D), 1) // HEAD == iota((256, D), 0) // 16
    masked = jnp.where(own_head, spread, 0.0).astype(BF16)
    keys_scr[...] = lax.dot_general(
        masked, wk[...], NT, preferred_element_type=F32
    ).astype(BF16)
    same = iota((256, 256), 1) // FIELDS == iota((256, 256), 0) % GROUP
    bias_scr[...] = jnp.where(same, 0.0, MASKED)


def merge_line(line, line_pixels, slot_w, keys_scr, bias_scr, normed_scr, pooled_scr):
    own_slot = iota((1, 16, 256), 2) // PIX == iota((1, 16, 256), 1)
    for part in range(4):
        pixels = line_pixels[line, :, 256 * part : 256 * part + 256][:COLS]
        spread = jnp.where(own_slot, pixels[:, None, :], 0.0).astype(BF16)
        tokens = dot(spread.reshape(COLS * 16, 256), slot_w[256 * part : 256 * part + 256, :])
        normed = layer_norm(tokens.astype(BF16).astype(F32)).astype(BF16)
        normed_scr[:, 16 * part : 16 * part + 16, :] = normed.reshape(COLS, 16, D)
    for quad in range(QUADS):
        normed = normed_scr[GROUP * quad : GROUP * quad + GROUP].reshape(GROUP * FIELDS, D)
        scores = lax.dot_general(keys_scr[...], normed, NT, preferred_element_type=F32)
        weights = softmax_rows(scores * EXP2_SCALE + bias_scr[...]).astype(BF16)
        pooled = dot(weights, normed).astype(BF16)
        start = pl.multiple_of(line * 48 + quad * 16, 16)
        pooled_scr[:, pl.ds(start, 16), :] = pooled.reshape(HEADS, 16, D)


def project(pooled_scr, wv, query_scr):
    halves = []
    for half in range(2):
        lane_head = iota((D, 256), 1) // HEAD
        value_w = wv[:, 256 * half : 256 * half + 256].astype(F32)
        total = jnp.zeros((2 * OWN, 256), F32)
        for head in range(8):
            masked = jnp.where(lane_head == head, value_w, 0.0).astype(BF16)
            total = total + dot(pooled_scr[8 * half + head], masked)
        halves.append(total)
    projected = jnp.concatenate(halves, axis=-1).reshape(ROWS * QUADS, 16, D)
    return projected + query_scr[...][None]


def last_quads(tokens):
    tokens = tokens.reshape(ROWS * QUADS, 8, D)
    return jnp.concatenate([tokens[QUADS * r + 2] for r in range(ROWS)], axis=0)


def with_last_column(tokens, quads):
    tokens = tokens.reshape(ROWS * QUADS, 8, D)
    is_last = iota((8, D), 0) % GROUP == GROUP - 1
    pieces = []
    for r in range(ROWS):
        own = tokens[QUADS * r + 2]
        pieces += [tokens[QUADS * r], tokens[QUADS * r + 1]]
        pieces += [jnp.where(is_last, quads[8 * r : 8 * r + 8], own)]
    return jnp.concatenate(pieces, axis=0)


def whole_kernel(
    ids_ref, shift_ref, window_ref, fields_ref, query_ref, embed_h, wk_h, wv_h, qkv_h, wo_h, out_ref,
    embed, wk, wv, qkv, wo, slot_w, keys_scr, bias_scr, normed_scr, pooled_scr, query_scr,
    stage, send, recv, line_pixels, latents, slab, edge_send, edge_recv, col_recv, up_recv, down_recv,
    encoded, back_edge_send, back_edge_recv, back_recv,
    load_sem, pix_send_sem, pix_recv_sem, col_send_sem, col_recv_sem, row_send_sem, row_recv_sem,
    back_send_sem, back_recv_sem,
):
    sector = lax.axis_index("var")
    sectors = lax.axis_size("var")
    band = lax.axis_index("lat")
    bands = lax.axis_size("lat")
    right = lax.rem(sector + 1, sectors)
    left = lax.rem(sector + sectors - 1, sectors)
    has_up = band > 0
    has_down = band < bands - 1

    barrier = pltpu.get_barrier_semaphore()
    for k in range(1, sectors):
        pl.semaphore_signal(
            barrier, inc=1, device_id={"var": lax.rem(sector + k, sectors)}, device_id_type=MESH
        )

    @pl.when(has_up)
    def _():
        pl.semaphore_signal(barrier, inc=1, device_id={"lat": band - 1}, device_id_type=MESH)

    @pl.when(has_down)
    def _():
        pl.semaphore_signal(barrier, inc=1, device_id={"lat": band + 1}, device_id_type=MESH)

    loads = [
        pltpu.make_async_copy(src, dst, load_sem.at[i])
        for i, (src, dst) in enumerate(
            [(embed_h, embed), (wk_h, wk), (wv_h, wv), (qkv_h, qkv), (wo_h, wo)]
        )
    ]
    for load in loads:
        load.start()

    pick_pixels(fields_ref[...], stage, send)

    @pl.when(jnp.logical_not(has_up))
    def _():
        up_recv[...] = jnp.zeros_like(up_recv)

    @pl.when(jnp.logical_not(has_down))
    def _():
        down_recv[...] = jnp.zeros_like(down_recv)

    neighbours = jnp.where(has_up, 1, 0) + jnp.where(has_down, 1, 0)
    pl.semaphore_wait(barrier, sectors - 1 + neighbours)

    def pixel_copy(piece, k, peer, slot):
        start, count = PIECES[piece]
        return remote(
            send.at[peer, pl.ds(start, count)], recv.at[slot, pl.ds(start, count)],
            pix_send_sem.at[piece, k], pix_recv_sem.at[piece, k], var=peer,
        )

    for piece in range(len(PIECES)):
        for k in SEND_ORDER:
            pixel_copy(piece, k, lax.rem(sector + k, sectors), sector).start()
    recv[sector] = send[sector]

    loads[0].wait()
    loads[1].wait()
    prepare_weights(
        ids_ref, shift_ref, embed, query_ref, wk, slot_w, keys_scr, bias_scr, query_scr
    )

    def take_piece(piece, lines):
        for k in range(1, sectors):
            source = lax.rem(sector + sectors - k, sectors)
            pixel_copy(piece, k, source, source).wait_recv()
        start, count = PIECES[piece]
        stage[:, start : start + count, :] = recv[:, start : start + count, :].astype(F32)
        for line in lines:
            for source in range(sectors):
                line_pixels[line, 0:COLS, 128 * source : 128 * source + 128] = stage[
                    source, COLS * line : COLS * line + COLS, :
                ]

    def one_line(line, carry):
        @pl.when(line == 0)
        def _():
            take_piece(0, (0,))

        @pl.when(line == 1)
        def _():
            take_piece(1, (1, 2, 3))

        @pl.when(line == 4)
        def _():
            take_piece(2, (4, 5))

        merge_line(line, line_pixels, slot_w, keys_scr, bias_scr, normed_scr, pooled_scr)
        return carry

    lax.fori_loop(0, ROWS, one_line, 0)

    loads[2].wait()
    fresh = project(pooled_scr, wv, query_scr)
    for pair in range(2):
        tokens = fresh[:, 8 * pair : 8 * pair + 8].reshape(OWN, D)
        latents[pair] = tokens.astype(BF16)
        if pair == 0:
            edge_send[...] = last_quads(tokens).astype(BF16)

    edge_out = remote(edge_send, edge_recv, col_send_sem.at[0], col_recv_sem.at[0], var=right)
    edge_out.start()
    col_out = remote(latents.at[1], col_recv, col_send_sem.at[1], col_recv_sem.at[1], var=left)
    col_out.start()

    def row_copies(pair):
        upward = remote(
            slab.at[pair, pl.ds(0, HALO)], down_recv.at[pair],
            row_send_sem.at[pair, 0], row_recv_sem.at[pair, 0], lat=band - 1,
        )
        downward = remote(
            slab.at[pair, pl.ds(OWN - HALO, HALO)], up_recv.at[pair],
            row_send_sem.at[pair, 1], row_recv_sem.at[pair, 1], lat=band + 1,
        )
        return upward, downward

    def send_rows(pair):
        upward, downward = row_copies(pair)

        @pl.when(has_up)
        def _():
            upward.start()

        @pl.when(has_down)
        def _():
            downward.start()

    def take_rows(pair):
        upward, downward = row_copies(pair)

        @pl.when(has_down)
        def _():
            upward.wait_recv()

        @pl.when(has_up)
        def _():
            downward.wait_recv()

    shift = jnp.minimum(shift_ref[0], shift_ref[1])
    column = column_of(iota((OWN, D), 0))
    edge_out.wait_recv()
    slab[0] = with_last_column(latents[0].astype(F32), edge_recv[...].astype(F32)).astype(BF16)
    send_rows(0)
    col_out.wait_recv()
    slab[1] = jnp.where(
        column < shift, col_recv[...].astype(F32), latents[1].astype(F32)
    ).astype(BF16)
    send_rows(1)

    first = band * ROWS - (WIN_LAT - 1)
    total_rows = window_ref.shape[0]
    key_token = iota((1, KEYS), 1)
    query_token = iota((OWN, 1), 0)
    key_row = jnp.full((1, KEYS), -1, jnp.int32)
    query_row = jnp.full((OWN, 1), -1, jnp.int32)
    for k in range(ROWS + 2 * (WIN_LAT - 1)):
        row = first + k
        inside = (row >= 0) & (row < total_rows)
        ident = jnp.where(inside, window_ref[jnp.clip(row, 0, total_rows - 1)], -1)
        key_row = jnp.where(key_token // LINE == k, ident, key_row)
        if 0 <= k - (WIN_LAT - 1) < ROWS:
            query_row = jnp.where(query_token // LINE == k - (WIN_LAT - 1), ident, query_row)

    loads[3].wait()
    loads[4].wait()
    for pair in range(2):
        def wrapped(token):
            if pair == 0:
                return jnp.where((column_of(token) == COLS - 1) & (sector == 0), 1, 0)
            return jnp.where((column_of(token) < shift) & (sector == sectors - 1), 1, 0)

        same = (query_row * 2 + wrapped(query_token)) == (key_row * 2 + wrapped(key_token))
        bias = jnp.where(same, 0.0, MASKED)
        own = slab[pair].astype(F32)
        take_rows(pair)
        up = up_recv[pair].astype(F32)[HALO - EDGE :]
        down = down_recv[pair].astype(F32)[:EDGE]
        normed = layer_norm(jnp.concatenate([up, own, down], axis=0))
        queries = dot(normed[EDGE : EDGE + OWN].astype(BF16), qkv[:, :D])
        normed = normed.astype(BF16)
        keys = dot(normed, qkv[:, D : 2 * D]).astype(BF16)
        values = dot(normed, qkv[:, 2 * D :]).astype(BF16)
        for part, (start, stop) in enumerate(QUERY_PARTS[pair]):
            mixed = attention(queries[start:stop], keys, values, bias[start:stop])
            done = own[start:stop] + dot(mixed, wo[...])
            encoded[pair, start:stop] = done.astype(BF16)
            if pair == 0:
                back_edge_send[...] = last_quads(done).astype(BF16)
                back_edge = remote(
                    back_edge_send, back_edge_recv, back_send_sem.at[0], back_recv_sem.at[0], var=left
                )
                back_edge.start()
                backs = [back_edge]
            else:
                back = remote(
                    encoded.at[1, pl.ds(start, stop - start)], back_recv.at[pl.ds(start, stop - start)],
                    back_send_sem.at[1 + part], back_recv_sem.at[1 + part], var=right,
                )
                back.start()
                backs.append(back)

    row = iota((192, OWN), 0)
    place = row // 16 % ROWS * LINE + row % 16 // GROUP * 8 + row // 96 * GROUP + row % GROUP
    place = jnp.where(row % 16 < COLS, place, -1)
    order = jnp.where(place == iota((192, OWN), 1), 1.0, 0.0).astype(BF16)

    def in_place(tokens):
        return dot(order, tokens.astype(BF16)).reshape(2, ROWS, 16, D)[:, :, :COLS]

    backs[0].wait_recv()
    first_pair = in_place(
        with_last_column(encoded[0].astype(F32), back_edge_recv[...].astype(F32))
    )
    backs[1].wait_recv()
    backs[2].wait_recv()
    second_pair = in_place(
        jnp.where(column < shift, back_recv[...].astype(F32), encoded[1].astype(F32))
    )
    swap = shift_ref[1] > shift_ref[0]
    out_ref[0:2] = jnp.where(swap, second_pair, first_pair).astype(BF16)
    out_ref[2:4] = jnp.where(swap, first_pair, second_pair).astype(BF16)

    for piece in range(len(PIECES)):
        for k in range(1, sectors):
            pixel_copy(piece, k, lax.rem(sector + k, sectors), sector).wait_send()
    edge_out.wait_send()
    col_out.wait_send()
    for pair in range(2):
        upward, downward = row_copies(pair)

        @pl.when(has_up)
        def _():
            upward.wait_send()

        @pl.when(has_down)
        def _():
            downward.wait_send()

    for back in backs:
        back.wait_send()


def shards(
    fields, field_ids, embed_w, lat_query, perc_wk, perc_wv, swin_qkv, swin_wo, row_window, lon_shift
):
    vmem = pl.BlockSpec(memory_space=pltpu.VMEM)
    smem = pl.BlockSpec(memory_space=pltpu.SMEM)
    hbm = pl.BlockSpec(memory_space=pl.ANY)
    return pl.pallas_call(
        whole_kernel,
        out_shape=jax.ShapeDtypeStruct((LEVELS, ROWS, COLS, D), BF16),
        in_specs=[smem] * 3 + [vmem] * 2 + [hbm] * 5,
        out_specs=vmem,
        scratch_shapes=[
            pltpu.VMEM((FIELDS, PIX, D), BF16),
            pltpu.VMEM((D, D), BF16),
            pltpu.VMEM((D, D), BF16),
            pltpu.VMEM((D, 3 * D), BF16),
            pltpu.VMEM((D, D), BF16),
            pltpu.VMEM((FIELDS * PIX, D), BF16),
            pltpu.VMEM((256, D), BF16),
            pltpu.VMEM((256, 256), F32),
            pltpu.VMEM((COLS, FIELDS, D), BF16),
            pltpu.VMEM((HEADS, 2 * OWN, D), BF16),
            pltpu.VMEM((16, D), F32),
            pltpu.VMEM((8, 80, 128), F32),
            pltpu.VMEM((8, 80, 128), BF16),
            pltpu.VMEM((8, 80, 128), BF16),
            pltpu.VMEM((ROWS, 16, FIELDS * PIX), F32),
            pltpu.VMEM((2, OWN, D), BF16),
            pltpu.VMEM((2, OWN, D), BF16),
            pltpu.VMEM((48, D), BF16),
            pltpu.VMEM((48, D), BF16),
            pltpu.VMEM((OWN, D), BF16),
            pltpu.VMEM((2, HALO, D), BF16),
            pltpu.VMEM((2, HALO, D), BF16),
            pltpu.VMEM((2, OWN, D), BF16),
            pltpu.VMEM((48, D), BF16),
            pltpu.VMEM((48, D), BF16),
            pltpu.VMEM((OWN, D), BF16),
            pltpu.SemaphoreType.DMA((5,)),
            pltpu.SemaphoreType.DMA((3, 8)),
            pltpu.SemaphoreType.DMA((3, 8)),
            pltpu.SemaphoreType.DMA((2,)),
            pltpu.SemaphoreType.DMA((2,)),
            pltpu.SemaphoreType.DMA((2, 2)),
            pltpu.SemaphoreType.DMA((2, 2)),
            pltpu.SemaphoreType.DMA((3,)),
            pltpu.SemaphoreType.DMA((3,)),
        ],
        compiler_params=pltpu.CompilerParams(
            vmem_limit_bytes=63 << 20, collective_id=0, has_side_effects=True
        ),
        name="whole",
    )(
        field_ids, lon_shift, row_window, fields, lat_query, embed_w, perc_wk, perc_wv, swin_qkv, swin_wo
    )


def solution(mesh):
    in_specs = (P("var", "lat", None), P(), P(), P(), P(), P(), P(), P(), P(), P())
    out_specs = P(None, "lat", "var", None)
    return jax.shard_map(shards, mesh=mesh, in_specs=in_specs, out_specs=out_specs, check_vma=False)
```

time: 134 us -> 69.3 us (0.52)
  the two profiles are of different devices: /device:TPU:31 before, /device:TPU:95 now
where the time goes in v1:
time: 69.3 us; the launch traced here: 69.1 us
  Pallas kernels  67.2 us (97%)
  local copies, waits for them, and re-layouts  1.94 us (3%)
    pallas_call x1, Pallas kernels, shards(): pl.pallas_call(whole_kernel, out_shape=jax.ShapeDtypeStruct((LEVELS, ROWS...  67.2 us
    pallas_call x1, local copies, waits for them, and re-layouts, shards(): pl.pallas_call(whole_kernel, out_shape=jax.ShapeDtypeStruct((LEVELS, ROWS...  1.94 us

profile of v1, /device:TPU:95, one launch (start us, length us, event | category | flops | bytes accessed | tf_op | source)
XLA Modules:
  0.0 69.1 jit_solution(3395152365560211710)
XLA Ops:
  0.0 67.2 %whole.1 = bf16[4,6,12,512]{3,2,1,0:T(8,128)(2,1)} custom-call(s32[64]{0:T(128)} %ids_ref.1, s32[2]{0:T(128)} %shift_ref.1, s32[384]{0:T(512)} %window_ref.1, bf16[8,24,384]{2,1,0:T(8,128)(2,1)} %fields_ref.1, bf16[4,512]{1,0:T(4,128)(2,1)} %query_ref.1, bf16[64,16,512]{2,1,0:T(8,128)(2,1)} %embed_h.1, bf16[512,512]{1,0:T(8,128)(2,1)} %wk_h.1, ...), custom_call_target="tpu_custom_call" | custom-call | tf_op jit(solution)/shard_map/whole/pallas_call | solution.py:446
  67.2 1.9 %copy.11 = bf16[4,6,12,512]{3,0,2,1:T(4,128)(2,1)} copy(bf16[4,6,12,512]{3,2,1,0:T(8,128)(2,1)} %whole.1) | data formatting | bytes 589824 | tf_op jit(solution)/shard_map/whole/pallas_call | solution.py:446

commit v2 on v1

--- a/solution.py
+++ b/solution.py
@@ -35,7 +35,7 @@
 MESH = pl.DeviceIdType.MESH
 PIECES = ((0, 16), (16, 32), (48, 32))
 SEND_ORDER = (4, 3, 5, 2, 6, 1, 7)
-QUERY_PARTS = (((0, OWN),), ((0, 96), (96, OWN)))
+QUERY_PARTS = (((0, 96), (96, OWN)), ((0, 96), (96, OWN)))
 
 
 def dot(a, b):
@@ -192,7 +192,7 @@
     stage, send, recv, line_pixels, latents, slab, edge_send, edge_recv, col_recv, up_recv, down_recv,
     encoded, back_edge_send, back_edge_recv, back_recv,
     load_sem, pix_send_sem, pix_recv_sem, col_send_sem, col_recv_sem, row_send_sem, row_recv_sem,
-    back_send_sem, back_recv_sem,
+    back_send_sem, back_recv_sem, relay, relay_send_sem, relay_recv_sem, hub_send_sem, unit_recv_sem,
 ):
     sector = lax.axis_index("var")
     sectors = lax.axis_size("var")
@@ -200,8 +200,20 @@
     bands = lax.axis_size("lat")
     right = lax.rem(sector + 1, sectors)
     left = lax.rem(sector + sectors - 1, sectors)
+    relayed = bands == 64
+    half_bands = bands // 2
+    hub_low, hub_high = half_bands - 1, half_bands
+    partner = lax.rem(band + half_bands, bands)
+    is_low = band < half_bands
+    is_hub = (band == hub_low) | (band == hub_high)
+    is_odd = lax.rem(band, 2) == 1
+    sends_on = is_odd == is_low
+    unit = lax.rem(band, half_bands) // 2
     has_up = band > 0
     has_down = band < bands - 1
+    if relayed:
+        has_up = has_up & (band != hub_high)
+        has_down = has_down & (band != hub_low)
 
     barrier = pltpu.get_barrier_semaphore()
     for k in range(1, sectors):
@@ -216,6 +228,25 @@
     @pl.when(has_down)
     def _():
         pl.semaphore_signal(barrier, inc=1, device_id={"lat": band + 1}, device_id_type=MESH)
+
+    greetings = sectors - 1 + jnp.where(has_up, 1, 0) + jnp.where(has_down, 1, 0)
+    if relayed:
+        pl.semaphore_signal(barrier, inc=1, device_id={"lat": partner}, device_id_type=MESH)
+        greetings = greetings + 1 + jnp.where(is_hub, half_bands - 1, 1)
+
+        @pl.when(jnp.logical_not(is_hub))
+        def _():
+            hub = jnp.where(is_low, hub_low, hub_high)
+            pl.semaphore_signal(barrier, inc=1, device_id={"lat": hub}, device_id_type=MESH)
+
+        def greet(other, carry):
+            other = other + jnp.where(band == hub_high, hub_high + 1, 0)
+            pl.semaphore_signal(barrier, inc=1, device_id={"lat": other}, device_id_type=MESH)
+            return carry
+
+        @pl.when(is_hub)
+        def _():
+            lax.fori_loop(0, half_bands - 1, greet, 0)
 
     loads = [
         pltpu.make_async_copy(src, dst, load_sem.at[i])
@@ -228,16 +259,15 @@
 
     pick_pixels(fields_ref[...], stage, send)
 
-    @pl.when(jnp.logical_not(has_up))
+    @pl.when(band == 0)
     def _():
         up_recv[...] = jnp.zeros_like(up_recv)
 
-    @pl.when(jnp.logical_not(has_down))
+    @pl.when(band == bands - 1)
     def _():
         down_recv[...] = jnp.zeros_like(down_recv)
 
-    neighbours = jnp.where(has_up, 1, 0) + jnp.where(has_down, 1, 0)
-    pl.semaphore_wait(barrier, sectors - 1 + neighbours)
+    pl.semaphore_wait(barrier, greetings)
 
     def pixel_copy(piece, k, peer, slot):
         start, count = PIECES[piece]
@@ -311,6 +341,49 @@
         )
         return upward, downward
 
+    def hub_copies(pair, upward):
+        copies = []
+        for block in range(8):
+            number = 8 * pair + block
+            helper = half_bands + 2 * number if upward else 2 * number + 1
+            helper = {hub_low: bands - 1, hub_high: 0}.get(helper, helper)
+            start = 16 * block + (0 if upward else OWN - HALO)
+            copies.append(
+                remote(
+                    slab.at[pair, pl.ds(start, 16)], relay, hub_send_sem.at[number], relay_recv_sem.at[0],
+                    lat=helper,
+                )
+            )
+        return copies
+
+    relay_pair, relay_start = unit // 8, pl.multiple_of(lax.rem(unit, 8) * 16, 16)
+    relay_on = remote(relay, relay, relay_send_sem.at[0], relay_recv_sem.at[0], lat=partner)
+
+    def relay_in(landing, number, start, pair, hub):
+        return remote(
+            relay, landing.at[pair, pl.ds(start, 16)],
+            relay_send_sem.at[0], unit_recv_sem.at[number], lat=hub,
+        )
+
+    def relay_first(pair):
+        @pl.when(sends_on & jnp.logical_not(is_hub) & (relay_pair == pair))
+        def _():
+            relay_on.wait_recv()
+            relay_on.start()
+
+    def relay_second(pair):
+        @pl.when(jnp.logical_not(sends_on) & (relay_pair == pair))
+        def _():
+            relay_on.wait_recv()
+
+            @pl.when(is_low)
+            def _():
+                relay_in(down_recv, unit, relay_start, relay_pair, hub_low).start()
+
+            @pl.when(jnp.logical_not(is_low))
+            def _():
+                relay_in(up_recv, unit, relay_start, relay_pair, hub_high).start()
+
     def send_rows(pair):
         upward, downward = row_copies(pair)
 
@@ -322,6 +395,17 @@
         def _():
             downward.start()
 
+        if relayed:
+            @pl.when(band == hub_low)
+            def _():
+                for copy in hub_copies(pair, False):
+                    copy.start()
+
+            @pl.when(band == hub_high)
+            def _():
+                for copy in hub_copies(pair, True):
+                    copy.start()
+
     def take_rows(pair):
         upward, downward = row_copies(pair)
 
@@ -332,17 +416,33 @@
         @pl.when(has_up)
         def _():
             downward.wait_recv()
+
+        if relayed:
+            @pl.when(band == hub_low)
+            def _():
+                for block in range(8):
+                    relay_in(down_recv, 8 * pair + block, 16 * block, pair, hub_low).wait_recv()
+
+            @pl.when(band == hub_high)
+            def _():
+                for block in range(8):
+                    relay_in(up_recv, 8 * pair + block, 16 * block, pair, hub_high).wait_recv()
 
     shift = jnp.minimum(shift_ref[0], shift_ref[1])
     column = column_of(iota((OWN, D), 0))
     edge_out.wait_recv()
     slab[0] = with_last_column(latents[0].astype(F32), edge_recv[...].astype(F32)).astype(BF16)
     send_rows(0)
+    if relayed:
+        relay_first(0)
     col_out.wait_recv()
     slab[1] = jnp.where(
         column < shift, col_recv[...].astype(F32), latents[1].astype(F32)
     ).astype(BF16)
     send_rows(1)
+    if relayed:
+        relay_second(0)
+        relay_first(1)
 
     first = band * ROWS - (WIN_LAT - 1)
     total_rows = window_ref.shape[0]
@@ -381,7 +481,12 @@
             mixed = attention(queries[start:stop], keys, values, bias[start:stop])
             done = own[start:stop] + dot(mixed, wo[...])
             encoded[pair, start:stop] = done.astype(BF16)
+            if relayed and pair == 0 and part == 0:
+                relay_second(1)
+            if pair == 0 and part == 0:
+                continue
             if pair == 0:
+                done = encoded[0].astype(F32)
                 back_edge_send[...] = last_quads(done).astype(BF16)
                 back_edge = remote(
                     back_edge_send, back_edge_recv, back_send_sem.at[0], back_recv_sem.at[0], var=left
@@ -396,26 +501,23 @@
                 back.start()
                 backs.append(back)
 
-    row = iota((192, OWN), 0)
-    place = row // 16 % ROWS * LINE + row % 16 // GROUP * 8 + row // 96 * GROUP + row % GROUP
-    place = jnp.where(row % 16 < COLS, place, -1)
-    order = jnp.where(place == iota((192, OWN), 1), 1.0, 0.0).astype(BF16)
-
-    def in_place(tokens):
-        return dot(order, tokens.astype(BF16)).reshape(2, ROWS, 16, D)[:, :, :COLS]
-
+    swap = jnp.where(shift_ref[1] > shift_ref[0], 1, 0)
+    row = iota((2 * OWN, OWN), 0)
+    level = row % LEVELS
+    place = row // 48 * LINE + row % 48 // 16 * 8 + level % 2 * GROUP + row % 16 // LEVELS
+    hit = place == iota((2 * OWN, OWN), 1)
+    orders = [
+        jnp.where(hit & (level // 2 == (swap if pair == 0 else 1 - swap)), 1.0, 0.0).astype(BF16)
+        for pair in range(2)
+    ]
     backs[0].wait_recv()
-    first_pair = in_place(
-        with_last_column(encoded[0].astype(F32), back_edge_recv[...].astype(F32))
-    )
+    first_pair = with_last_column(encoded[0].astype(F32), back_edge_recv[...].astype(F32))
+    result = dot(orders[0], first_pair.astype(BF16))
     backs[1].wait_recv()
     backs[2].wait_recv()
-    second_pair = in_place(
-        jnp.where(column < shift, back_recv[...].astype(F32), encoded[1].astype(F32))
-    )
-    swap = shift_ref[1] > shift_ref[0]
-    out_ref[0:2] = jnp.where(swap, second_pair, first_pair).astype(BF16)
-    out_ref[2:4] = jnp.where(swap, first_pair, second_pair).astype(BF16)
+    second_pair = jnp.where(column < shift, back_recv[...].astype(F32), encoded[1].astype(F32))
+    result = result + dot(orders[1], second_pair.astype(BF16))
+    out_ref[...] = result.reshape(ROWS, COLS, LEVELS, D).astype(BF16)
 
     for piece in range(len(PIECES)):
         for k in range(1, sectors):
@@ -433,6 +535,21 @@
         def _():
             downward.wait_send()
 
+    if relayed:
+        @pl.when(band == hub_low)
+        def _():
+            for copy in hub_copies(0, False) + hub_copies(1, False):
+                copy.wait_send()
+
+        @pl.when(band == hub_high)
+        def _():
+            for copy in hub_copies(0, True) + hub_copies(1, True):
+                copy.wait_send()
+
+        @pl.when(jnp.logical_not(sends_on & is_hub))
+        def _():
+            relay_on.wait_send()
+
     for back in backs:
         back.wait_send()
 
@@ -443,9 +560,9 @@
     vmem = pl.BlockSpec(memory_space=pltpu.VMEM)
     smem = pl.BlockSpec(memory_space=pltpu.SMEM)
     hbm = pl.BlockSpec(memory_space=pl.ANY)
-    return pl.pallas_call(
+    encoded = pl.pallas_call(
         whole_kernel,
-        out_shape=jax.ShapeDtypeStruct((LEVELS, ROWS, COLS, D), BF16),
+        out_shape=jax.ShapeDtypeStruct((ROWS, COLS, LEVELS, D), BF16),
         in_specs=[smem] * 3 + [vmem] * 2 + [hbm] * 5,
         out_specs=vmem,
         scratch_shapes=[
@@ -484,6 +601,11 @@
             pltpu.SemaphoreType.DMA((2, 2)),
             pltpu.SemaphoreType.DMA((3,)),
             pltpu.SemaphoreType.DMA((3,)),
+            pltpu.VMEM((16, D), BF16),
+            pltpu.SemaphoreType.DMA((1,)),
+            pltpu.SemaphoreType.DMA((1,)),
+            pltpu.SemaphoreType.DMA((16,)),
+            pltpu.SemaphoreType.DMA((16,)),
         ],
         compiler_params=pltpu.CompilerParams(
             vmem_limit_bytes=63 << 20, collective_id=0, has_side_effects=True
@@ -492,6 +614,7 @@
     )(
         field_ids, lon_shift, row_window, fields, lat_query, embed_w, perc_wk, perc_wv, swin_qkv, swin_wo
     )
+    return jnp.transpose(encoded, (2, 0, 1, 3))
 
 
 def solution(mesh):

time: 69.3 us -> 70.4 us (1.016)
  the two profiles are of different devices: /device:TPU:95 before, /device:TPU:31 now
where the time goes in v2:
time: 70.4 us; the launch traced here: 70.2 us
  Pallas kernels  68.5 us (97%)
  local copies, waits for them, and re-layouts  1.78 us (3%)
    pallas_call x1, Pallas kernels, shards(): pl.pallas_call(whole_kernel, out_shape=jax.ShapeDtypeStruct((ROWS, COLS,...  68.5 us
    unnamed x1, local copies, waits for them, and re-layouts  1.78 us

profile of v2, /device:TPU:31, one launch (start us, length us, event | category | flops | bytes accessed | tf_op | source)
XLA Modules:
  0.0 70.2 jit_solution(1724838843479970173)
XLA Ops:
  0.0 68.5 %whole.1 = bf16[6,12,4,512]{3,2,1,0:T(4,128)(2,1)} custom-call(s32[64]{0:T(128)} %ids_ref.1, s32[2]{0:T(128)} %shift_ref.1, s32[384]{0:T(512)} %window_ref.1, bf16[8,24,384]{2,1,0:T(8,128)(2,1)} %fields_ref.1, bf16[4,512]{1,0:T(4,128)(2,1)} %query_ref.1, bf16[64,16,512]{2,1,0:T(8,128)(2,1)} %embed_h.1, bf16[512,512]{1,0:T(8,128)(2,1)} %wk_h.1, ...), custom_call_target="tpu_custom_call" | custom-call | tf_op jit(solution)/shard_map/whole/pallas_call | solution.py:563
  68.5 1.8 %copy.12 = bf16[4,6,12,512]{3,0,2,1:T(4,128)(2,1)} copy(bf16[4,6,12,512]{3,0,2,1:T(4,128)(2,1)} %bitcast.1) | data formatting | bytes 589824

commit v3 on v1

v3 whole, which is shorter than its diff:
```python
import functools
import math

import jax
import jax.numpy as jnp
from jax import lax
from jax.experimental import pallas as pl
from jax.experimental.pallas import tpu as pltpu
from jax.sharding import PartitionSpec as P

D = 512
HEADS = 16
HEAD = 32
LEVELS = 4
PATCH = 4
WIN_LAT = 6
WIN_LON = 12
FIELDS = 64
ROWS = 6
COLS = 12
PIX = PATCH * PATCH
GROUP = 4
QUADS = COLS // GROUP
LINE = 2 * COLS
OWN = ROWS * LINE
HALO = 128
KEYS = 384
EDGE = 120

EPSILON = 1e-05
MASKED = -1e30
EXP2_SCALE = math.log2(math.e) / math.sqrt(HEAD)
F32 = jnp.float32
BF16 = jnp.bfloat16
NT = (((1,), (1,)), ((), ()))
MESH = pl.DeviceIdType.MESH
SEND_ORDER = (4, 3, 5, 2, 6, 1, 7)
CHUNKS = 3
EMBED_STEP = 2
MERGE_STEP = 3
CHUNK = 2 * LINE
UP_PARTS = ((0, 48), (48, 48), (96, 32))
DOWN_PARTS = ((16, 32), (48, 48), (96, 48))


def dot(a, b):
    return jnp.dot(a, b, preferred_element_type=F32)


def iota(shape, dim):
    return lax.broadcasted_iota(jnp.int32, shape, dim)


def layer_norm(values):
    row_mean = jnp.sum(values, axis=-1, keepdims=True) * (1.0 / D)
    centred = values - row_mean
    variance = jnp.sum(centred * centred, axis=-1, keepdims=True) * (1.0 / D)
    return centred * lax.rsqrt(variance + EPSILON)


def softmax_rows(scores):
    row_top = jnp.max(scores, axis=-1, keepdims=True)
    lifted = jnp.exp2(scores - row_top)
    return lifted * (1.0 / jnp.sum(lifted, axis=-1, keepdims=True))


def column_of(token):
    return (token % LINE) // 8 * GROUP + token % GROUP


def remote(src, dst, send_sem, recv_sem, **device):
    return pltpu.make_async_remote_copy(
        src_ref=src, dst_ref=dst, send_sem=send_sem, recv_sem=recv_sem,
        device_id=device, device_id_type=MESH,
    )


def start_copy(copy):
    copy.start()


def wait_received(copy):
    copy.wait_recv()


def wait_sent(copy):
    copy.wait_send()


def attention(queries, keys, values, bias):
    count, key_count = queries.shape[0], keys.shape[0]
    lane_head = iota((count, 256), 1) // HEAD
    halves = []
    for half in range(2):
        cut = slice(256 * half, 256 * half + 256)
        part = queries[:, cut]
        stacked = jnp.concatenate(
            [jnp.where(lane_head == h, part, 0.0).astype(BF16) for h in range(8)], axis=0
        )
        scores = lax.dot_general(stacked, keys[:, cut], NT, preferred_element_type=F32)
        scores = scores.reshape(8, count, key_count) * EXP2_SCALE + bias[None]
        weights = softmax_rows(scores).astype(BF16).reshape(8 * count, key_count)
        mixed = dot(weights, values[:, cut]).reshape(8, count, 256)
        total = jnp.zeros((count, 256), F32)
        for h in range(8):
            total = jnp.where(lane_head == h, mixed[h], total)
        halves.append(total.astype(BF16))
    return jnp.concatenate(halves, axis=-1)


def pick_pixels(fields, stage, send):
    flat = fields.astype(F32).reshape(8 * ROWS * PATCH, 384).astype(BF16)
    row = iota((512, 1), 0)
    column = row % 16
    source = jnp.where(column < COLS, (row % 128) // 16 * 48 + column * PATCH + row // 128, -1)
    pick = jnp.where(source == iota((512, 384), 1), 1.0, 0.0).astype(BF16)
    turned = lax.dot_general(pick, flat, NT, preferred_element_type=F32).astype(BF16)
    row = iota((192, 1), 0)
    target = (row // PATCH) % ROWS * 128 + row // (ROWS * PATCH) * PIX + row % PATCH * PATCH
    lane = iota((192, 768), 1)
    total = jnp.zeros((128, 768), F32)
    for j in range(PATCH):
        place = jnp.where(target + j == lane, 1.0, 0.0).astype(BF16)
        total = total + dot(turned[128 * j : 128 * j + 128], place)
    for sector in range(8):
        stage[sector, 72:80, :] = jnp.zeros((8, 128), F32)
        for line in range(ROWS):
            stage[sector, COLS * line : COLS * line + COLS, :] = total[
                16 * sector : 16 * sector + COLS, 128 * line : 128 * line + 128
            ]
    send[...] = stage[...].astype(BF16)


def prepare_weights(ids_ref, shift_ref, embed, query_ref, wk, slot_w, keys_scr, bias_scr, query_scr):
    def place(slot, carry):
        start = pl.multiple_of(slot * PIX, PIX)
        slot_w[pl.ds(start, PIX), :] = embed[ids_ref[slot]]
        return carry

    lax.fori_loop(0, FIELDS, place, 0)
    swap = shift_ref[1] > shift_ref[0]
    query = query_ref[...].astype(F32)
    swapped = jnp.concatenate([query[2:], query[:2]], axis=0)
    query = jnp.where(swap, swapped, query)
    level = (iota((256, D), 0) // GROUP) % LEVELS
    spread = jnp.zeros((256, D), F32)
    for lev in range(LEVELS):
        spread = jnp.where(level == lev, query[lev : lev + 1, :], spread)
    query_scr[...] = spread[:16]
    own_head = iota((256, D), 1) // HEAD == iota((256, D), 0) // 16
    masked = jnp.where(own_head, spread, 0.0).astype(BF16)
    keys_scr[...] = lax.dot_general(
        masked, wk[...], NT, preferred_element_type=F32
    ).astype(BF16)
    same = iota((256, 256), 1) // FIELDS == iota((256, 256), 0) % GROUP
    bias_scr[...] = jnp.where(same, 0.0, MASKED)


def embed_line(line, part, line_pixels, slot_w, normed_scr):
    own_slot = iota((1, 16, 256), 2) // PIX == iota((1, 16, 256), 1)
    pixels = line_pixels[line][:COLS]
    spread = jnp.where(own_slot, pixels[:, None, :], 0.0).astype(BF16)
    weight = slot_w[pl.ds(pl.multiple_of(256 * part, 256), 256), :]
    tokens = dot(spread.reshape(COLS * 16, 256), weight)
    normed = layer_norm(tokens.astype(BF16).astype(F32)).astype(BF16)
    slots = pl.ds(pl.multiple_of(16 * part, 16), 16)
    normed_scr[pl.ds(line * COLS, COLS), slots, :] = normed.reshape(COLS, 16, D)


def merge_quad(quad, keys_scr, bias_scr, normed_scr, pooled_scr):
    normed = normed_scr[pl.ds(quad * GROUP, GROUP)].reshape(GROUP * FIELDS, D)
    scores = lax.dot_general(keys_scr[...], normed, NT, preferred_element_type=F32)
    weights = softmax_rows(scores * EXP2_SCALE + bias_scr[...]).astype(BF16)
    pooled = dot(weights, normed).astype(BF16)
    start = pl.multiple_of(quad * 16, 16)
    pooled_scr[:, pl.ds(start, 16), :] = pooled.reshape(HEADS, 16, D)


def project(chunk, pooled_scr, wv, query_scr):
    start = pl.multiple_of(chunk * 2 * CHUNK, 2 * CHUNK)
    halves = []
    for half in range(2):
        lane_head = iota((D, 256), 1) // HEAD
        value_w = wv[:, 256 * half : 256 * half + 256].astype(F32)
        total = jnp.zeros((2 * CHUNK, 256), F32)
        for head in range(8):
            masked = jnp.where(lane_head == head, value_w, 0.0).astype(BF16)
            total = total + dot(pooled_scr[8 * half + head, pl.ds(start, 2 * CHUNK), :], masked)
        halves.append(total)
    projected = jnp.concatenate(halves, axis=-1).reshape(2 * QUADS, 16, D)
    return projected + query_scr[...][None]


def quads_of(tokens, last):
    width = tokens.shape[-1]
    tokens = tokens.reshape(tokens.shape[0] // 8, 8, width)
    picked = [q for q in range(tokens.shape[0]) if (q % QUADS == QUADS - 1) == last]
    return jnp.concatenate([tokens[q] for q in picked], axis=0)


def with_last_column(rest, own, received):
    is_last = iota(own.shape, 0) % GROUP == GROUP - 1
    last = jnp.where(is_last, received, own)
    pieces = []
    for r in range(own.shape[0] // 8):
        pieces += [rest[16 * r : 16 * r + 16], last[8 * r : 8 * r + 8]]
    return jnp.concatenate(pieces, axis=0)


def whole_kernel(
    ids_ref, shift_ref, window_ref, fields_ref, query_ref, embed_h, wk_h, wv_h, qkv_h, wo_h, out_ref,
    embed, wk, wv, qkv, wo, slot_w, keys_scr, bias_scr, normed_scr, pooled_scr, query_scr,
    stage, send, recv, line_pixels, latents, slab, edge_send, edge_recv, col_recv, up_recv, down_recv,
    encoded, back_edge_recv, back_recv,
    load_sem, pix_send_sem, pix_recv_sem, col_send_sem, col_recv_sem, row_send_sem, row_recv_sem,
    back_send_sem, back_recv_sem, extra_up, extra_down, extra_send_sem, extra_recv_sem,
):
    sector = lax.axis_index("var")
    sectors = lax.axis_size("var")
    band = lax.axis_index("lat")
    bands = lax.axis_size("lat")
    right = lax.rem(sector + 1, sectors)
    left = lax.rem(sector + sectors - 1, sectors)
    is_first = sector == 0
    is_last = sector == sectors - 1
    is_end = is_first | is_last
    has_left = jnp.logical_not(is_first)
    has_right = jnp.logical_not(is_last)
    has_up = band > 0
    has_down = band < bands - 1

    barrier = pltpu.get_barrier_semaphore()
    for k in range(1, sectors):
        pl.semaphore_signal(
            barrier, inc=1, device_id={"var": lax.rem(sector + k, sectors)}, device_id_type=MESH
        )

    @pl.when(has_up)
    def _():
        pl.semaphore_signal(barrier, inc=1, device_id={"lat": band - 1}, device_id_type=MESH)

    @pl.when(has_down)
    def _():
        pl.semaphore_signal(barrier, inc=1, device_id={"lat": band + 1}, device_id_type=MESH)

    loads = [
        pltpu.make_async_copy(src, dst, load_sem.at[i])
        for i, (src, dst) in enumerate(
            [(embed_h, embed), (wk_h, wk), (wv_h, wv), (qkv_h, qkv), (wo_h, wo)]
        )
    ]
    for load in loads:
        load.start()

    pick_pixels(fields_ref[...], stage, send)

    @pl.when(jnp.logical_not(has_up))
    def _():
        up_recv[...] = jnp.zeros_like(up_recv)

    @pl.when(jnp.logical_not(has_down))
    def _():
        down_recv[...] = jnp.zeros_like(down_recv)

    @pl.when((band == 0) & is_end)
    def _():
        extra_up[...] = jnp.zeros_like(extra_up)

    @pl.when((band == bands - 1) & is_end)
    def _():
        extra_down[...] = jnp.zeros_like(extra_down)

    @pl.when(is_first)
    def _():
        edge_recv[...] = jnp.zeros_like(edge_recv)

    @pl.when(is_last)
    def _():
        col_recv[...] = jnp.zeros_like(col_recv)

    neighbours = jnp.where(has_up, 1, 0) + jnp.where(has_down, 1, 0)
    pl.semaphore_wait(barrier, sectors - 1 + neighbours)

    def pixel_copy(k, peer, slot):
        return remote(
            send.at[peer], recv.at[slot], pix_send_sem.at[k], pix_recv_sem.at[k], var=peer
        )

    for k in SEND_ORDER:
        pixel_copy(k, lax.rem(sector + k, sectors), sector).start()
    recv[sector] = send[sector]

    loads[0].wait()
    loads[1].wait()
    prepare_weights(
        ids_ref, shift_ref, embed, query_ref, wk, slot_w, keys_scr, bias_scr, query_scr
    )

    def one_part(turn, carry):
        own = sector // 2
        part = lax.rem(own // 2 + turn // 2, 2) * 2 + lax.rem(own % 2 + turn % 2, 2)
        for side in range(2):
            source = part * 2 + side

            @pl.when(source != sector)
            def _():
                pixel_copy(lax.rem(sector + sectors - source, sectors), source, source).wait_recv()

            stage[side] = recv[source].astype(F32)
            for line in range(ROWS):
                line_pixels[line, 0:COLS, 128 * side : 128 * side + 128] = stage[
                    side, COLS * line : COLS * line + COLS, :
                ]

        def lines(step, carry):
            for k in range(EMBED_STEP):
                embed_line(step * EMBED_STEP + k, part, line_pixels, slot_w, normed_scr)
            return carry

        lax.fori_loop(0, ROWS // EMBED_STEP, lines, 0)
        return carry

    lax.fori_loop(0, 4, one_part, 0)

    shift = jnp.minimum(shift_ref[0], shift_ref[1])

    def column_copies(chunk):
        quads = pl.ds(pl.multiple_of(chunk * 16, 16), 16)
        tokens = pl.ds(pl.multiple_of(chunk * CHUNK, 16), CHUNK)
        return (
            remote(
                edge_send.at[quads], edge_recv.at[quads],
                col_send_sem.at[0, chunk], col_recv_sem.at[0, chunk], var=right,
            ),
            remote(
                latents.at[1, tokens], col_recv.at[tokens],
                col_send_sem.at[1, chunk], col_recv_sem.at[1, chunk], var=left,
            ),
        )

    def extra_copies(chunk):
        quads = pl.ds(pl.multiple_of(chunk * 16, 16), 16)
        tokens = pl.ds(pl.multiple_of(chunk * CHUNK, 16), CHUNK)
        copies = []
        for end, src, part in ((is_first, latents.at[1, tokens], tokens), (is_last, edge_send.at[quads], quads)):
            copies.append((end & has_up, remote(
                src, extra_down.at[part], extra_send_sem.at[0, chunk], extra_recv_sem.at[0, chunk], lat=band - 1
            )))
            copies.append((end & has_down, remote(
                src, extra_up.at[part], extra_send_sem.at[1, chunk], extra_recv_sem.at[1, chunk], lat=band + 1
            )))
        return copies

    def take_extra():
        for chunk in range(CHUNKS):
            for i, (_, copy) in enumerate(extra_copies(chunk)):
                end = is_first if i < 2 else is_last
                pl.when(end & (has_down if i % 2 == 0 else has_up))(functools.partial(wait_received, copy))

    def row_copies(pair, chunk):
        (up_start, up_count), (down_start, down_count) = UP_PARTS[chunk], DOWN_PARTS[chunk]
        up_part, down_part = pl.ds(up_start, up_count), pl.ds(down_start, down_count)
        upward = remote(
            slab.at[pair, up_part], down_recv.at[pair, up_part],
            row_send_sem.at[pair, 0, chunk], row_recv_sem.at[pair, 0, chunk], lat=band - 1,
        )
        downward = remote(
            slab.at[pair, down_part], up_recv.at[pair, down_part],
            row_send_sem.at[pair, 1, chunk], row_recv_sem.at[pair, 1, chunk], lat=band + 1,
        )
        return upward, downward

    def send_rows(pair, chunk):
        upward, downward = row_copies(pair, chunk)

        @pl.when(has_up)
        def _():
            upward.start()

        @pl.when(has_down)
        def _():
            downward.start()

    def take_rows(pair):
        for chunk in range(CHUNKS):
            upward, downward = row_copies(pair, chunk)

            @pl.when(has_down)
            def _():
                upward.wait_recv()

            @pl.when(has_up)
            def _():
                downward.wait_recv()

    def share_rows(chunk):
        edge_copy, col_copy = column_copies(chunk)
        tokens = slice(CHUNK * chunk, CHUNK * chunk + CHUNK)
        quads = slice(16 * chunk, 16 * chunk + 16)
        pl.when(has_right)(lambda: wait_received(col_copy))
        column = column_of(iota((CHUNK, D), 0))
        slab[1, tokens] = jnp.where(
            column < shift, col_recv[tokens].astype(F32), latents[1, tokens].astype(F32)
        ).astype(BF16)
        send_rows(1, chunk)
        pl.when(has_left)(lambda: wait_received(edge_copy))
        own = latents[0, tokens].astype(F32)
        slab[0, tokens] = with_last_column(
            quads_of(own, False), quads_of(own, True), edge_recv[quads].astype(F32)
        ).astype(BF16)
        send_rows(0, chunk)

    loads[2].wait()

    def one_chunk(chunk, carry):
        def quads(step, carry):
            for k in range(MERGE_STEP):
                quad = chunk * 2 * QUADS + step * MERGE_STEP + k
                merge_quad(quad, keys_scr, bias_scr, normed_scr, pooled_scr)
            return carry

        lax.fori_loop(0, 2 * QUADS // MERGE_STEP, quads, 0)
        fresh = project(chunk, pooled_scr, wv, query_scr)
        start = pl.multiple_of(chunk * CHUNK, 16)
        for pair in range(2):
            tokens = fresh[:, 8 * pair : 8 * pair + 8].reshape(CHUNK, D)
            latents[pair, pl.ds(start, CHUNK), :] = tokens.astype(BF16)
            if pair == 0:
                quads = pl.ds(pl.multiple_of(chunk * 16, 16), 16)
                edge_send[quads, :] = quads_of(tokens, True).astype(BF16)
        edge_copy, col_copy = column_copies(chunk)
        pl.when(has_right)(lambda: start_copy(edge_copy))
        pl.when(has_left)(lambda: start_copy(col_copy))
        for where, copy in extra_copies(chunk):
            pl.when(where)(functools.partial(start_copy, copy))
        for ready in range(CHUNKS - 1):
            @pl.when(chunk == ready + 1)
            def _():
                share_rows(ready)

        return carry

    lax.fori_loop(0, CHUNKS, one_chunk, 0)
    share_rows(CHUNKS - 1)

    first = band * ROWS - (WIN_LAT - 1)
    total_rows = window_ref.shape[0]

    def row_ident(k):
        row = first + k
        inside = (row >= 0) & (row < total_rows)
        return jnp.where(inside, window_ref[jnp.clip(row, 0, total_rows - 1)], -1)

    key_token = iota((1, KEYS), 1)
    query_token = iota((OWN, 1), 0)
    key_row = jnp.full((1, KEYS), -1, jnp.int32)
    query_row = jnp.full((OWN, 1), -1, jnp.int32)
    for k in range(ROWS + 2 * (WIN_LAT - 1)):
        ident = row_ident(k)
        key_row = jnp.where(key_token // LINE == k, ident, key_row)
        if 0 <= k - (WIN_LAT - 1) < ROWS:
            query_row = jnp.where(query_token // LINE == k - (WIN_LAT - 1), ident, query_row)

    loads[3].wait()
    loads[4].wait()
    def around(own_part, halo_part):
        edge = halo_part.shape[0] // 2
        return jnp.concatenate([halo_part[:edge], own_part, halo_part[edge:]], axis=0).astype(BF16)

    def attend_extra(own, up, down, same):
        own_qkv = dot(layer_norm(own).astype(BF16), qkv[...])
        halo = jnp.concatenate([up.astype(F32), down.astype(F32)], axis=0)
        halo = dot(layer_norm(halo).astype(BF16), qkv[:, D:])
        keys = around(own_qkv[:, D : 2 * D], halo[:, :D])
        values = around(own_qkv[:, 2 * D :], halo[:, D:])
        mixed = attention(own_qkv[:, :D], keys, values, jnp.where(same, 0.0, MASKED))
        return (own + dot(mixed, wo[...])).astype(BF16)

    take_extra()

    @pl.when(is_first)
    def _():
        below = [jnp.where(column_of(token) < shift, 1, 0) for token in (query_token, key_token)]
        same = (query_row * 2 + below[0]) == (key_row * 2 + below[1])
        back_recv[...] = attend_extra(
            latents[1].astype(F32), extra_up[OWN - EDGE :], extra_down[:EDGE], same
        )

    @pl.when(is_last)
    def _():
        ident = [jnp.full((48, 1), -1, jnp.int32), jnp.full((1, 128), -1, jnp.int32)]
        token = [iota((48, 1), 0), iota((1, 128), 1)]
        for k in range(ROWS + 2 * (WIN_LAT - 1)):
            ident[1] = jnp.where(token[1] // 8 == k, row_ident(k), ident[1])
            ident[0] = jnp.where(token[0] // 8 == k - (WIN_LAT - 1), row_ident(k), ident[0])
        side = [jnp.where(t % GROUP == GROUP - 1, 1, 0) for t in token]
        same = (ident[0] * 2 + side[0]) == (ident[1] * 2 + side[1])
        back_edge_recv[...] = attend_extra(
            edge_send[...].astype(F32), extra_up[0:48].astype(F32)[8:], extra_down[0:48].astype(F32)[:40], same
        )

    own_parts = []
    for pair in range(2):
        own = slab[pair].astype(F32)
        own_parts.append((own, dot(layer_norm(own).astype(BF16), qkv[...])))

    def windows(pair):
        def wrapped(token):
            if pair == 0:
                return jnp.where((column_of(token) == COLS - 1) & (sector == 0), 1, 0)
            return jnp.where((column_of(token) < shift) & (sector == sectors - 1), 1, 0)

        same = (query_row * 2 + wrapped(query_token)) == (key_row * 2 + wrapped(key_token))
        bias = jnp.where(same, 0.0, MASKED)
        own, own_qkv = own_parts[pair]
        take_rows(pair)
        halo = jnp.concatenate(
            [up_recv[pair].astype(F32)[OWN - EDGE :], down_recv[pair].astype(F32)[:EDGE]], axis=0
        )
        halo = dot(layer_norm(halo).astype(BF16), qkv[:, D:])

        keys = around(own_qkv[:, D : 2 * D], halo[:, :D])
        values = around(own_qkv[:, 2 * D :], halo[:, D:])
        return own, own_qkv[:, :D], keys, values, bias

    backs = []
    own, queries, keys, values, bias = windows(1)
    for part, (start, stop) in enumerate(((0, 96), (96, OWN))):
        mixed = attention(queries[start:stop], keys, values, bias[start:stop])
        encoded[1, start:stop] = (own[start:stop] + dot(mixed, wo[...])).astype(BF16)
        back = remote(
            encoded.at[1, pl.ds(start, stop - start)], back_recv.at[pl.ds(start, stop - start)],
            back_send_sem.at[part], back_recv_sem.at[part], var=right,
        )
        pl.when(has_right)(functools.partial(start_copy, back))
        backs.append(back)

    own, queries, keys, values, bias = windows(0)
    for part, last in enumerate((True, False)):
        mixed = attention(quads_of(queries, last), keys, values, quads_of(bias, last))
        done = quads_of(own, last) + dot(mixed, wo[...])
        if last:
            encoded[0, 0:48] = done.astype(BF16)
            back = remote(
                encoded.at[0, pl.ds(0, 48)], back_edge_recv,
                back_send_sem.at[2], back_recv_sem.at[2], var=left,
            )
            pl.when(has_left)(functools.partial(start_copy, back))
            backs.append(back)
        else:
            first_rest = done

    swap = jnp.where(shift_ref[1] > shift_ref[0], 1, 0)
    row = iota((2 * OWN, OWN), 0)
    level = row % LEVELS
    place = row // 48 * LINE + row % 48 // 16 * 8 + level % 2 * GROUP + row % 16 // LEVELS
    hit = place == iota((2 * OWN, OWN), 1)
    orders = [
        jnp.where(hit & (level // 2 == (swap if pair == 0 else 1 - swap)), 1.0, 0.0).astype(BF16)
        for pair in range(2)
    ]
    pl.when(has_right)(lambda: wait_received(backs[2]))
    first_pair = with_last_column(
        first_rest, encoded[0, 0:48].astype(F32), back_edge_recv[...].astype(F32)
    )
    result = dot(orders[0], first_pair.astype(BF16))
    pl.when(has_left)(lambda: wait_received(backs[0]))
    pl.when(has_left)(lambda: wait_received(backs[1]))
    column = column_of(iota((OWN, D), 0))
    second_pair = jnp.where(column < shift, back_recv[...].astype(F32), encoded[1].astype(F32))
    result = result + dot(orders[1], second_pair.astype(BF16))
    out_ref[...] = result.reshape(ROWS, COLS, LEVELS, D).astype(BF16)

    for k in range(1, sectors):
        pixel_copy(k, lax.rem(sector + k, sectors), sector).wait_send()
    for chunk in range(CHUNKS):
        edge_copy, col_copy = column_copies(chunk)
        pl.when(has_right)(functools.partial(wait_sent, edge_copy))
        pl.when(has_left)(functools.partial(wait_sent, col_copy))
        for where, copy in extra_copies(chunk):
            pl.when(where)(functools.partial(wait_sent, copy))
        for pair in range(2):
            upward, downward = row_copies(pair, chunk)

            @pl.when(has_up)
            def _():
                upward.wait_send()

            @pl.when(has_down)
            def _():
                downward.wait_send()

    for back, where in zip(backs, (has_right, has_right, has_left)):
        pl.when(where)(functools.partial(wait_sent, back))


def shards(
    fields, field_ids, embed_w, lat_query, perc_wk, perc_wv, swin_qkv, swin_wo, row_window, lon_shift
):
    vmem = pl.BlockSpec(memory_space=pltpu.VMEM)
    smem = pl.BlockSpec(memory_space=pltpu.SMEM)
    hbm = pl.BlockSpec(memory_space=pl.ANY)
    encoded = pl.pallas_call(
        whole_kernel,
        out_shape=jax.ShapeDtypeStruct((ROWS, COLS, LEVELS, D), BF16),
        in_specs=[smem] * 3 + [vmem] * 2 + [hbm] * 5,
        out_specs=vmem,
        scratch_shapes=[
            pltpu.VMEM((FIELDS, PIX, D), BF16),
            pltpu.VMEM((D, D), BF16),
            pltpu.VMEM((D, D), BF16),
            pltpu.VMEM((D, 3 * D), BF16),
            pltpu.VMEM((D, D), BF16),
            pltpu.VMEM((FIELDS * PIX, D), BF16),
            pltpu.VMEM((256, D), BF16),
            pltpu.VMEM((256, 256), F32),
            pltpu.VMEM((ROWS * COLS, FIELDS, D), BF16),
            pltpu.VMEM((HEADS, 2 * OWN, D), BF16),
            pltpu.VMEM((16, D), F32),
            pltpu.VMEM((8, 80, 128), F32),
            pltpu.VMEM((8, 80, 128), BF16),
            pltpu.VMEM((8, 80, 128), BF16),
            pltpu.VMEM((ROWS, 16, 256), F32),
            pltpu.VMEM((2, OWN, D), BF16),
            pltpu.VMEM((2, OWN, D), BF16),
            pltpu.VMEM((48, D), BF16),
            pltpu.VMEM((48, D), BF16),
            pltpu.VMEM((OWN, D), BF16),
            pltpu.VMEM((2, OWN, D), BF16),
            pltpu.VMEM((2, OWN, D), BF16),
            pltpu.VMEM((2, OWN, D), BF16),
            pltpu.VMEM((48, D), BF16),
            pltpu.VMEM((OWN, D), BF16),
            pltpu.SemaphoreType.DMA((5,)),
            pltpu.SemaphoreType.DMA((8,)),
            pltpu.SemaphoreType.DMA((8,)),
            pltpu.SemaphoreType.DMA((2, CHUNKS)),
            pltpu.SemaphoreType.DMA((2, CHUNKS)),
            pltpu.SemaphoreType.DMA((2, 2, CHUNKS)),
            pltpu.SemaphoreType.DMA((2, 2, CHUNKS)),
            pltpu.SemaphoreType.DMA((3,)),
            pltpu.SemaphoreType.DMA((3,)),
            pltpu.VMEM((OWN, D), BF16),
            pltpu.VMEM((OWN, D), BF16),
            pltpu.SemaphoreType.DMA((2, CHUNKS)),
            pltpu.SemaphoreType.DMA((2, CHUNKS)),
        ],
        compiler_params=pltpu.CompilerParams(
            vmem_limit_bytes=63 << 20, collective_id=0, has_side_effects=True
        ),
        name="whole",
    )(
        field_ids, lon_shift, row_window, fields, lat_query, embed_w, perc_wk, perc_wv, swin_qkv, swin_wo
    )
    return jnp.transpose(encoded, (2, 0, 1, 3))


def solution(mesh):
    in_specs = (P("var", "lat", None), P(), P(), P(), P(), P(), P(), P(), P(), P())
    out_specs = P(None, "lat", "var", None)
    return jax.shard_map(shards, mesh=mesh, in_specs=in_specs, out_specs=out_specs, check_vma=False)
```

time: 69.3 us -> 64 us (0.924)
  the two profiles are of different devices: /device:TPU:95 before, /device:TPU:31 now
where the time goes in v3:
time: 64 us; the launch traced here: 63.8 us
  Pallas kernels  62 us (97%)
  local copies, waits for them, and re-layouts  1.78 us (3%)
    pallas_call x1, Pallas kernels, shards(): pl.pallas_call(whole_kernel, out_shape=jax.ShapeDtypeStruct((ROWS, COLS,...  62 us
    unnamed x1, local copies, waits for them, and re-layouts  1.78 us

profile of v3, /device:TPU:31, one launch (start us, length us, event | category | flops | bytes accessed | tf_op | source)
XLA Modules:
  0.0 63.8 jit_solution(10807167391076880329)
XLA Ops:
  0.0 62.0 %whole.1 = bf16[6,12,4,512]{3,2,1,0:T(4,128)(2,1)} custom-call(s32[64]{0:T(128)} %ids_ref.1, s32[2]{0:T(128)} %shift_ref.1, s32[384]{0:T(512)} %window_ref.1, bf16[8,24,384]{2,1,0:T(8,128)(2,1)} %fields_ref.1, bf16[4,512]{1,0:T(4,128)(2,1)} %query_ref.1, bf16[64,16,512]{2,1,0:T(8,128)(2,1)} %embed_h.1, bf16[512,512]{1,0:T(8,128)(2,1)} %wk_h.1, ...), custom_call_target="tpu_custom_call" | custom-call | tf_op jit(solution)/shard_map/whole/pallas_call | solution.py:603
  62.0 1.8 %copy.12 = bf16[4,6,12,512]{3,0,2,1:T(4,128)(2,1)} copy(bf16[4,6,12,512]{3,0,2,1:T(4,128)(2,1)} %bitcast.1) | data formatting | bytes 589824

commit v4 on v3

--- a/solution.py
+++ b/solution.py
@@ -36,8 +36,9 @@
 MESH = pl.DeviceIdType.MESH
 SEND_ORDER = (4, 3, 5, 2, 6, 1, 7)
 CHUNKS = 3
-EMBED_STEP = 2
-MERGE_STEP = 3
+EMBED_STEP = 6
+MERGE_STEP = 6
+NEAR = 128
 CHUNK = 2 * LINE
 UP_PARTS = ((0, 48), (48, 48), (96, 32))
 DOWN_PARTS = ((16, 32), (48, 48), (96, 48))
@@ -105,6 +106,61 @@
         for h in range(8):
             total = jnp.where(lane_head == h, mixed[h], total)
         halves.append(total.astype(BF16))
+    return jnp.concatenate(halves, axis=-1)
+
+
+def heads_apart(queries):
+    lane_head = iota(queries.shape, 1) // HEAD
+    return jnp.concatenate(
+        [jnp.where(lane_head == h, queries, 0.0).astype(BF16) for h in range(8)], axis=0
+    )
+
+
+def heads_together(stacked):
+    lane_head = iota((stacked.shape[1], 256), 1) // HEAD
+    total = jnp.broadcast_to(stacked[0], lane_head.shape)
+    for h in range(1, 8):
+        total = jnp.where(lane_head == h, stacked[h], total)
+    return total
+
+
+def attend_near(queries, keys, values, bias):
+    count, key_count = bias.shape
+    state = []
+    for half in range(2):
+        cut = slice(256 * half, 256 * half + 256)
+        scores = lax.dot_general(
+            heads_apart(queries[:, cut]), keys[:, cut], NT, preferred_element_type=F32
+        )
+        scores = scores.reshape(8, count, key_count) * EXP2_SCALE + bias[None]
+        top = jnp.max(scores, axis=-1, keepdims=True)
+        lifted = jnp.exp2(scores - top)
+        total = jnp.sum(lifted, axis=-1, keepdims=True)
+        mixed = dot(lifted.astype(BF16).reshape(8 * count, key_count), values[:, cut])
+        state.append((top, total, heads_together(mixed.reshape(8, count, 256))))
+    return state
+
+
+def attend_far(queries, keys, values, bias, state):
+    count, key_count = bias.shape
+    halves = []
+    for half, (near_top, near_total, near_mixed) in enumerate(state):
+        cut = slice(256 * half, 256 * half + 256)
+        scores = lax.dot_general(
+            heads_apart(queries[:, cut]), keys[:, cut], NT, preferred_element_type=F32
+        )
+        scores = scores.reshape(8, count, key_count) * EXP2_SCALE + bias[None]
+        top = jnp.maximum(near_top, jnp.max(scores, axis=-1, keepdims=True))
+        lifted = jnp.exp2(scores - top)
+        near_scale = jnp.exp2(near_top - top)
+        total = near_scale * near_total + jnp.sum(lifted, axis=-1, keepdims=True)
+        inverse = 1.0 / total
+        mixed = dot(
+            (lifted * inverse).astype(BF16).reshape(8 * count, key_count), values[:, cut]
+        )
+        mixed = heads_together(mixed.reshape(8, count, 256))
+        mixed = mixed + near_mixed * heads_together(near_scale * inverse)
+        halves.append(mixed.astype(BF16))
     return jnp.concatenate(halves, axis=-1)
 
 
@@ -476,6 +532,26 @@
         mixed = attention(own_qkv[:, :D], keys, values, jnp.where(same, 0.0, MASKED))
         return (own + dot(mixed, wo[...])).astype(BF16)
 
+    def window_bias(pair):
+        def wrapped(token):
+            if pair == 0:
+                return jnp.where((column_of(token) == COLS - 1) & (sector == 0), 1, 0)
+            return jnp.where((column_of(token) < shift) & (sector == sectors - 1), 1, 0)
+
+        same = (query_row * 2 + wrapped(query_token)) == (key_row * 2 + wrapped(key_token))
+        return jnp.where(same, 0.0, MASKED)
+
+    near = {}
+    for pair in (1, 0):
+        own = slab[pair].astype(F32)
+        own_qkv = dot(layer_norm(own).astype(BF16), qkv[...])
+        queries, keys, values = own_qkv[:, :D], own_qkv[:, D : 2 * D], own_qkv[:, 2 * D :]
+        bias = window_bias(pair)
+        state = attend_near(
+            queries, keys[:NEAR].astype(BF16), values[:NEAR].astype(BF16), bias[:, EDGE : EDGE + NEAR]
+        )
+        near[pair] = own, queries, keys[NEAR:], values[NEAR:], state
+
     take_extra()
 
     @pl.when(is_first)
@@ -499,56 +575,42 @@
             edge_send[...].astype(F32), extra_up[0:48].astype(F32)[8:], extra_down[0:48].astype(F32)[:40], same
         )
 
-    own_parts = []
-    for pair in range(2):
-        own = slab[pair].astype(F32)
-        own_parts.append((own, dot(layer_norm(own).astype(BF16), qkv[...])))
-
-    def windows(pair):
+    def attend_window(pair):
+        own, queries, keys, values, state = near[pair]
+        take_rows(pair)
+        halo = jnp.concatenate(
+            [up_recv[pair].astype(F32)[OWN - EDGE :], down_recv[pair].astype(F32)[:EDGE]], axis=0
+        )
+        halo = dot(layer_norm(halo).astype(BF16), qkv[:, D:])
+        keys, values = around(keys, halo[:, :D]), around(values, halo[:, D:])
+        far_token = iota((1, 2 * EDGE + OWN - NEAR), 1)
+        far_token = jnp.where(far_token < EDGE, far_token, far_token + NEAR)
+        far_row = jnp.full(far_token.shape, -1, jnp.int32)
+        for k in range(ROWS + 2 * (WIN_LAT - 1)):
+            far_row = jnp.where(far_token // LINE == k, row_ident(k), far_row)
+
         def wrapped(token):
             if pair == 0:
                 return jnp.where((column_of(token) == COLS - 1) & (sector == 0), 1, 0)
             return jnp.where((column_of(token) < shift) & (sector == sectors - 1), 1, 0)
 
-        same = (query_row * 2 + wrapped(query_token)) == (key_row * 2 + wrapped(key_token))
-        bias = jnp.where(same, 0.0, MASKED)
-        own, own_qkv = own_parts[pair]
-        take_rows(pair)
-        halo = jnp.concatenate(
-            [up_recv[pair].astype(F32)[OWN - EDGE :], down_recv[pair].astype(F32)[:EDGE]], axis=0
-        )
-        halo = dot(layer_norm(halo).astype(BF16), qkv[:, D:])
-
-        keys = around(own_qkv[:, D : 2 * D], halo[:, :D])
-        values = around(own_qkv[:, 2 * D :], halo[:, D:])
-        return own, own_qkv[:, :D], keys, values, bias
+        same = (query_row * 2 + wrapped(query_token)) == (far_row * 2 + wrapped(far_token))
+        mixed = attend_far(queries, keys, values, jnp.where(same, 0.0, MASKED), state)
+        return own + dot(mixed, wo[...])
 
     backs = []
-    own, queries, keys, values, bias = windows(1)
-    for part, (start, stop) in enumerate(((0, 96), (96, OWN))):
-        mixed = attention(queries[start:stop], keys, values, bias[start:stop])
-        encoded[1, start:stop] = (own[start:stop] + dot(mixed, wo[...])).astype(BF16)
-        back = remote(
-            encoded.at[1, pl.ds(start, stop - start)], back_recv.at[pl.ds(start, stop - start)],
-            back_send_sem.at[part], back_recv_sem.at[part], var=right,
-        )
-        pl.when(has_right)(functools.partial(start_copy, back))
-        backs.append(back)
-
-    own, queries, keys, values, bias = windows(0)
-    for part, last in enumerate((True, False)):
-        mixed = attention(quads_of(queries, last), keys, values, quads_of(bias, last))
-        done = quads_of(own, last) + dot(mixed, wo[...])
-        if last:
-            encoded[0, 0:48] = done.astype(BF16)
-            back = remote(
-                encoded.at[0, pl.ds(0, 48)], back_edge_recv,
-                back_send_sem.at[2], back_recv_sem.at[2], var=left,
-            )
-            pl.when(has_left)(functools.partial(start_copy, back))
-            backs.append(back)
-        else:
-            first_rest = done
+    encoded[1] = attend_window(1).astype(BF16)
+    back = remote(encoded.at[1], back_recv, back_send_sem.at[0], back_recv_sem.at[0], var=right)
+    pl.when(has_right)(functools.partial(start_copy, back))
+    backs.append(back)
+    done = attend_window(0)
+    encoded[0, 0:48] = quads_of(done, True).astype(BF16)
+    back = remote(
+        encoded.at[0, pl.ds(0, 48)], back_edge_recv, back_send_sem.at[1], back_recv_sem.at[1], var=left
+    )
+    pl.when(has_left)(functools.partial(start_copy, back))
+    backs.append(back)
+    first_rest = quads_of(done, False)
 
     swap = jnp.where(shift_ref[1] > shift_ref[0], 1, 0)
     row = iota((2 * OWN, OWN), 0)
@@ -559,13 +621,12 @@
         jnp.where(hit & (level // 2 == (swap if pair == 0 else 1 - swap)), 1.0, 0.0).astype(BF16)
         for pair in range(2)
     ]
-    pl.when(has_right)(lambda: wait_received(backs[2]))
+    pl.when(has_right)(lambda: wait_received(backs[1]))
     first_pair = with_last_column(
         first_rest, encoded[0, 0:48].astype(F32), back_edge_recv[...].astype(F32)
     )
     result = dot(orders[0], first_pair.astype(BF16))
     pl.when(has_left)(lambda: wait_received(backs[0]))
-    pl.when(has_left)(lambda: wait_received(backs[1]))
     column = column_of(iota((OWN, D), 0))
     second_pair = jnp.where(column < shift, back_recv[...].astype(F32), encoded[1].astype(F32))
     result = result + dot(orders[1], second_pair.astype(BF16))
@@ -590,7 +651,7 @@
             def _():
                 downward.wait_send()
 
-    for back, where in zip(backs, (has_right, has_right, has_left)):
+    for back, where in zip(backs, (has_right, has_left)):
         pl.when(where)(functools.partial(wait_sent, back))
 
 
@@ -638,8 +699,8 @@
             pltpu.SemaphoreType.DMA((2, CHUNKS)),
             pltpu.SemaphoreType.DMA((2, 2, CHUNKS)),
             pltpu.SemaphoreType.DMA((2, 2, CHUNKS)),
-            pltpu.SemaphoreType.DMA((3,)),
-            pltpu.SemaphoreType.DMA((3,)),
+            pltpu.SemaphoreType.DMA((2,)),
+            pltpu.SemaphoreType.DMA((2,)),
             pltpu.VMEM((OWN, D), BF16),
             pltpu.VMEM((OWN, D), BF16),
             pltpu.SemaphoreType.DMA((2, CHUNKS)),

time: 64 us -> 61.6 us (0.963)
  Pallas kernels: 62 us -> 59.7 us
    pallas_call x1, Pallas kernels: 62 us -> 59.7 us  [shards(): pl.pallas_call(whole_kernel, out_shape=jax.ShapeDtypeStruct((ROWS, COLS,...]
where the time goes in v4:
time: 61.6 us; the launch traced here: 61.4 us
  Pallas kernels  59.7 us (97%)
  local copies, waits for them, and re-layouts  1.78 us (3%)
    pallas_call x1, Pallas kernels, shards(): pl.pallas_call(whole_kernel, out_shape=jax.ShapeDtypeStruct((ROWS, COLS,...  59.7 us
    unnamed x1, local copies, waits for them, and re-layouts  1.78 us

profile of v4, /device:TPU:31, one launch (start us, length us, event | category | flops | bytes accessed | tf_op | source)
XLA Modules:
  0.0 61.4 jit_solution(333965820822484268)
XLA Ops:
  0.0 59.7 %whole.1 = bf16[6,12,4,512]{3,2,1,0:T(4,128)(2,1)} custom-call(s32[64]{0:T(128)} %ids_ref.1, s32[2]{0:T(128)} %shift_ref.1, s32[384]{0:T(512)} %window_ref.1, bf16[8,24,384]{2,1,0:T(8,128)(2,1)} %fields_ref.1, bf16[4,512]{1,0:T(4,128)(2,1)} %query_ref.1, bf16[64,16,512]{2,1,0:T(8,128)(2,1)} %embed_h.1, bf16[512,512]{1,0:T(8,128)(2,1)} %wk_h.1, ...), custom_call_target="tpu_custom_call" | custom-call | tf_op jit(solution)/shard_map/whole/pallas_call | solution.py:664
  59.7 1.8 %copy.12 = bf16[4,6,12,512]{3,0,2,1:T(4,128)(2,1)} copy(bf16[4,6,12,512]{3,0,2,1:T(4,128)(2,1)} %bitcast.1) | data formatting | bytes 589824

commit v5 on v4

--- a/solution.py
+++ b/solution.py
@@ -107,6 +107,14 @@
             total = jnp.where(lane_head == h, mixed[h], total)
         halves.append(total.astype(BF16))
     return jnp.concatenate(halves, axis=-1)
+
+
+def split_values(wv, value_scr):
+    lane_head = iota((D, 256), 1) // HEAD
+    for half in range(2):
+        value_w = wv[:, 256 * half : 256 * half + 256].astype(F32)
+        for head in range(8):
+            value_scr[8 * half + head] = jnp.where(lane_head == head, value_w, 0.0).astype(BF16)
 
 
 def heads_apart(queries):
@@ -218,7 +226,7 @@
     spread = jnp.where(own_slot, pixels[:, None, :], 0.0).astype(BF16)
     weight = slot_w[pl.ds(pl.multiple_of(256 * part, 256), 256), :]
     tokens = dot(spread.reshape(COLS * 16, 256), weight)
-    normed = layer_norm(tokens.astype(BF16).astype(F32)).astype(BF16)
+    normed = layer_norm(tokens).astype(BF16)
     slots = pl.ds(pl.multiple_of(16 * part, 16), 16)
     normed_scr[pl.ds(line * COLS, COLS), slots, :] = normed.reshape(COLS, 16, D)
 
@@ -232,16 +240,13 @@
     pooled_scr[:, pl.ds(start, 16), :] = pooled.reshape(HEADS, 16, D)
 
 
-def project(chunk, pooled_scr, wv, query_scr):
+def project(chunk, pooled_scr, value_scr, query_scr):
     start = pl.multiple_of(chunk * 2 * CHUNK, 2 * CHUNK)
     halves = []
     for half in range(2):
-        lane_head = iota((D, 256), 1) // HEAD
-        value_w = wv[:, 256 * half : 256 * half + 256].astype(F32)
         total = jnp.zeros((2 * CHUNK, 256), F32)
-        for head in range(8):
-            masked = jnp.where(lane_head == head, value_w, 0.0).astype(BF16)
-            total = total + dot(pooled_scr[8 * half + head, pl.ds(start, 2 * CHUNK), :], masked)
+        for head in range(8 * half, 8 * half + 8):
+            total = total + dot(pooled_scr[head, pl.ds(start, 2 * CHUNK), :], value_scr[head])
         halves.append(total)
     projected = jnp.concatenate(halves, axis=-1).reshape(2 * QUADS, 16, D)
     return projected + query_scr[...][None]
@@ -270,6 +275,7 @@
     encoded, back_edge_recv, back_recv,
     load_sem, pix_send_sem, pix_recv_sem, col_send_sem, col_recv_sem, row_send_sem, row_recv_sem,
     back_send_sem, back_recv_sem, extra_up, extra_down, extra_send_sem, extra_recv_sem,
+    value_scr,
 ):
     sector = lax.axis_index("var")
     sectors = lax.axis_size("var")
@@ -351,6 +357,8 @@
     prepare_weights(
         ids_ref, shift_ref, embed, query_ref, wk, slot_w, keys_scr, bias_scr, query_scr
     )
+    loads[2].wait()
+    split_values(wv, value_scr)
 
     def one_part(turn, carry):
         own = sector // 2
@@ -466,7 +474,6 @@
         ).astype(BF16)
         send_rows(0, chunk)
 
-    loads[2].wait()
 
     def one_chunk(chunk, carry):
         def quads(step, carry):
@@ -476,7 +483,7 @@
             return carry
 
         lax.fori_loop(0, 2 * QUADS // MERGE_STEP, quads, 0)
-        fresh = project(chunk, pooled_scr, wv, query_scr)
+        fresh = project(chunk, pooled_scr, value_scr, query_scr)
         start = pl.multiple_of(chunk * CHUNK, 16)
         for pair in range(2):
             tokens = fresh[:, 8 * pair : 8 * pair + 8].reshape(CHUNK, D)
@@ -660,7 +667,7 @@
 ):
     vmem = pl.BlockSpec(memory_space=pltpu.VMEM)
     smem = pl.BlockSpec(memory_space=pltpu.SMEM)
-    hbm = pl.BlockSpec(memory_space=pl.ANY)
+    hbm = pl.BlockSpec(memory_space=pltpu.HBM)
     encoded = pl.pallas_call(
         whole_kernel,
         out_shape=jax.ShapeDtypeStruct((ROWS, COLS, LEVELS, D), BF16),
@@ -705,6 +712,7 @@
             pltpu.VMEM((OWN, D), BF16),
             pltpu.SemaphoreType.DMA((2, CHUNKS)),
             pltpu.SemaphoreType.DMA((2, CHUNKS)),
+            pltpu.VMEM((HEADS, D, 256), BF16),
         ],
         compiler_params=pltpu.CompilerParams(
             vmem_limit_bytes=63 << 20, collective_id=0, has_side_effects=True

time: 61.6 us -> 60.8 us (0.987)
  Pallas kernels: 59.7 us -> 58.8 us
    pallas_call x1, Pallas kernels: 59.7 us -> 58.8 us  [shards(): pl.pallas_call(whole_kernel, out_shape=jax.ShapeDtypeStruct((ROWS, COLS,...]
where the time goes in v5:
time: 60.8 us; the launch traced here: 60.6 us
  Pallas kernels  58.8 us (97%)
  local copies, waits for them, and re-layouts  1.78 us (3%)
    pallas_call x1, Pallas kernels, shards(): pl.pallas_call(whole_kernel, out_shape=jax.ShapeDtypeStruct((ROWS, COLS,...  58.8 us
    unnamed x1, local copies, waits for them, and re-layouts  1.78 us

profile of v5, /device:TPU:31, one launch (start us, length us, event | category | flops | bytes accessed | tf_op | source)
XLA Modules:
  0.0 60.6 jit_solution(14658358329298418638)
XLA Ops:
  0.0 58.8 %whole.1 = bf16[6,12,4,512]{3,2,1,0:T(4,128)(2,1)} custom-call(s32[64]{0:T(128)} %ids_ref.1, s32[2]{0:T(128)} %shift_ref.1, s32[384]{0:T(512)} %window_ref.1, bf16[8,24,384]{2,1,0:T(8,128)(2,1)} %fields_ref.1, bf16[4,512]{1,0:T(4,128)(2,1)} %query_ref.1, bf16[64,16,512]{2,1,0:T(8,128)(2,1)} %embed_h.1, bf16[512,512]{1,0:T(8,128)(2,1)} %wk_h.1, ...), custom_call_target="tpu_custom_call" | custom-call | tf_op jit(solution)/shard_map/whole/pallas_call | solution.py:671
  58.8 1.8 %copy.12 = bf16[4,6,12,512]{3,0,2,1:T(4,128)(2,1)} copy(bf16[4,6,12,512]{3,0,2,1:T(4,128)(2,1)} %bitcast.1) | data formatting | bytes 589824

commit v6 on v5

--- a/solution.py
+++ b/solution.py
@@ -33,6 +33,7 @@
 F32 = jnp.float32
 BF16 = jnp.bfloat16
 NT = (((1,), (1,)), ((), ()))
+TN = (((0,), (0,)), ((), ()))
 MESH = pl.DeviceIdType.MESH
 SEND_ORDER = (4, 3, 5, 2, 6, 1, 7)
 CHUNKS = 3
@@ -214,9 +215,9 @@
     own_head = iota((256, D), 1) // HEAD == iota((256, D), 0) // 16
     masked = jnp.where(own_head, spread, 0.0).astype(BF16)
     keys_scr[...] = lax.dot_general(
-        masked, wk[...], NT, preferred_element_type=F32
+        wk[...], masked, NT, preferred_element_type=F32
     ).astype(BF16)
-    same = iota((256, 256), 1) // FIELDS == iota((256, 256), 0) % GROUP
+    same = iota((256, 256), 0) // FIELDS == iota((256, 256), 1) % GROUP
     bias_scr[...] = jnp.where(same, 0.0, MASKED)
 
 
@@ -233,9 +234,10 @@
 
 def merge_quad(quad, keys_scr, bias_scr, normed_scr, pooled_scr):
     normed = normed_scr[pl.ds(quad * GROUP, GROUP)].reshape(GROUP * FIELDS, D)
-    scores = lax.dot_general(keys_scr[...], normed, NT, preferred_element_type=F32)
-    weights = softmax_rows(scores * EXP2_SCALE + bias_scr[...]).astype(BF16)
-    pooled = dot(weights, normed).astype(BF16)
+    scores = dot(normed, keys_scr[...]) * EXP2_SCALE + bias_scr[...]
+    lifted = jnp.exp2(scores - jnp.max(scores, axis=0, keepdims=True))
+    weights = (lifted * (1.0 / jnp.sum(lifted, axis=0, keepdims=True))).astype(BF16)
+    pooled = lax.dot_general(weights, normed, TN, preferred_element_type=F32).astype(BF16)
     start = pl.multiple_of(quad * 16, 16)
     pooled_scr[:, pl.ds(start, 16), :] = pooled.reshape(HEADS, 16, D)
 
@@ -680,7 +682,7 @@
             pltpu.VMEM((D, 3 * D), BF16),
             pltpu.VMEM((D, D), BF16),
             pltpu.VMEM((FIELDS * PIX, D), BF16),
-            pltpu.VMEM((256, D), BF16),
+            pltpu.VMEM((D, 256), BF16),
             pltpu.VMEM((256, 256), F32),
             pltpu.VMEM((ROWS * COLS, FIELDS, D), BF16),
             pltpu.VMEM((HEADS, 2 * OWN, D), BF16),

time: 60.8 us -> 59.5 us (0.979)
  Pallas kernels: 58.8 us -> 57.6 us
    pallas_call x1, Pallas kernels: 58.8 us -> 57.6 us  [shards(): pl.pallas_call(whole_kernel, out_shape=jax.ShapeDtypeStruct((ROWS, COLS,...]
where the time goes in v6:
time: 59.5 us; the launch traced here: 59.4 us
  Pallas kernels  57.6 us (97%)
  local copies, waits for them, and re-layouts  1.78 us (3%)
    pallas_call x1, Pallas kernels, shards(): pl.pallas_call(whole_kernel, out_shape=jax.ShapeDtypeStruct((ROWS, COLS,...  57.6 us
    unnamed x1, local copies, waits for them, and re-layouts  1.78 us

profile of v6, /device:TPU:31, one launch (start us, length us, event | category | flops | bytes accessed | tf_op | source)
XLA Modules:
  0.0 59.4 jit_solution(14620414586518037169)
XLA Ops:
  0.0 57.6 %whole.1 = bf16[6,12,4,512]{3,2,1,0:T(4,128)(2,1)} custom-call(s32[64]{0:T(128)} %ids_ref.1, s32[2]{0:T(128)} %shift_ref.1, s32[384]{0:T(512)} %window_ref.1, bf16[8,24,384]{2,1,0:T(8,128)(2,1)} %fields_ref.1, bf16[4,512]{1,0:T(4,128)(2,1)} %query_ref.1, bf16[64,16,512]{2,1,0:T(8,128)(2,1)} %embed_h.1, bf16[512,512]{1,0:T(8,128)(2,1)} %wk_h.1, ...), custom_call_target="tpu_custom_call" | custom-call | tf_op jit(solution)/shard_map/whole/pallas_call | solution.py:673
  57.6 1.8 %copy.12 = bf16[4,6,12,512]{3,0,2,1:T(4,128)(2,1)} copy(bf16[4,6,12,512]{3,0,2,1:T(4,128)(2,1)} %bitcast.1) | data formatting | bytes 589824

commit v7 on v6

--- a/solution.py
+++ b/solution.py
@@ -35,7 +35,7 @@
 NT = (((1,), (1,)), ((), ()))
 TN = (((0,), (0,)), ((), ()))
 MESH = pl.DeviceIdType.MESH
-SEND_ORDER = (4, 3, 5, 2, 6, 1, 7)
+SEND_ORDER = (7, 1, 6, 2, 5, 3, 4)
 CHUNKS = 3
 EMBED_STEP = 6
 MERGE_STEP = 6
@@ -506,8 +506,6 @@
         return carry
 
     lax.fori_loop(0, CHUNKS, one_chunk, 0)
-    share_rows(CHUNKS - 1)
-
     first = band * ROWS - (WIN_LAT - 1)
     total_rows = window_ref.shape[0]
 
@@ -550,14 +548,15 @@
         same = (query_row * 2 + wrapped(query_token)) == (key_row * 2 + wrapped(key_token))
         return jnp.where(same, 0.0, MASKED)
 
+    biases = [window_bias(pair)[:, EDGE : EDGE + NEAR] for pair in range(2)]
+    share_rows(CHUNKS - 1)
     near = {}
     for pair in (1, 0):
         own = slab[pair].astype(F32)
         own_qkv = dot(layer_norm(own).astype(BF16), qkv[...])
         queries, keys, values = own_qkv[:, :D], own_qkv[:, D : 2 * D], own_qkv[:, 2 * D :]
-        bias = window_bias(pair)
         state = attend_near(
-            queries, keys[:NEAR].astype(BF16), values[:NEAR].astype(BF16), bias[:, EDGE : EDGE + NEAR]
+            queries, keys[:NEAR].astype(BF16), values[:NEAR].astype(BF16), biases[pair]
         )
         near[pair] = own, queries, keys[NEAR:], values[NEAR:], state
 

time: 59.5 us -> 60.3 us (1.013)
  Pallas kernels: 57.6 us -> 58.4 us
    pallas_call x1, Pallas kernels: 57.6 us -> 58.4 us  [shards(): pl.pallas_call(whole_kernel, out_shape=jax.ShapeDtypeStruct((ROWS, COLS,...]
where the time goes in v7:
time: 60.3 us; the launch traced here: 60.2 us
  Pallas kernels  58.4 us (97%)
  local copies, waits for them, and re-layouts  1.78 us (3%)
    pallas_call x1, Pallas kernels, shards(): pl.pallas_call(whole_kernel, out_shape=jax.ShapeDtypeStruct((ROWS, COLS,...  58.4 us
    unnamed x1, local copies, waits for them, and re-layouts  1.78 us

profile of v7, /device:TPU:31, one launch (start us, length us, event | category | flops | bytes accessed | tf_op | source)
XLA Modules:
  0.0 60.2 jit_solution(11020310429213551098)
XLA Ops:
  0.0 58.4 %whole.1 = bf16[6,12,4,512]{3,2,1,0:T(4,128)(2,1)} custom-call(s32[64]{0:T(128)} %ids_ref.1, s32[2]{0:T(128)} %shift_ref.1, s32[384]{0:T(512)} %window_ref.1, bf16[8,24,384]{2,1,0:T(8,128)(2,1)} %fields_ref.1, bf16[4,512]{1,0:T(4,128)(2,1)} %query_ref.1, bf16[64,16,512]{2,1,0:T(8,128)(2,1)} %embed_h.1, bf16[512,512]{1,0:T(8,128)(2,1)} %wk_h.1, ...), custom_call_target="tpu_custom_call" | custom-call | tf_op jit(solution)/shard_map/whole/pallas_call | solution.py:672
  58.4 1.8 %copy.12 = bf16[4,6,12,512]{3,0,2,1:T(4,128)(2,1)} copy(bf16[4,6,12,512]{3,0,2,1:T(4,128)(2,1)} %bitcast.1) | data formatting | bytes 589824
